TPU v7x, 512 devices: a whole 4x8x8 slice. The times are simulated.
512 devices in a mesh: ctx: 32 (over z_lo, x, core), exp: 16 (over y, z_hi).
Axes of the slice: x: 4, y: 8, z: 8 (z_hi: 2, z_lo: 4; z = z_hi * 4 + z_lo), core: 2. Of those that a mesh axis runs over, the one named last changes fastest.
Arguments:
- tokens: bfloat16 [8192, 7168], P('ctx', 'exp'), may hold values from -6 to 6
- shared_gate: bfloat16 [7168, 2048], P('ctx', 'exp'), may hold values from -0.0625 to 0.0625
- shared_up: bfloat16 [7168, 2048], P('ctx', 'exp'), may hold values from -0.0625 to 0.0625
- shared_down: bfloat16 [2048, 7168], P(None, 'exp'), may hold values from -0.125 to 0.125
- expert_gate: bfloat16 [16, 7168, 2048], P('exp', 'ctx'), may hold values from -0.0625 to 0.0625
- expert_up: bfloat16 [16, 7168, 2048], P('exp', 'ctx'), may hold values from -0.0625 to 0.0625
- expert_down: bfloat16 [16, 2048, 7168], P('exp', None, 'ctx'), may hold values from -0.125 to 0.125
- hit_rows: int32 [32, 16, 6], P('ctx'), may hold values from 0 to 255, as said below
- hit_counts: int32 [32, 16], P('ctx'), may hold values from 1 to 6, 48 in all within a row
- hit_weights: float32 [32, 16, 6], P('ctx'), may hold values from 0.1 to 1
Outputs:
- mixed: bfloat16 [8192, 7168], P('ctx', 'exp')
Inputs may be any that keep to these rules, and one draw needn't show every extreme that they name: `hit_rows`: the 6 entries of one ctx shard and one expert are distinct token positions of that shard; entries from the shard's count on are to be ignored. `hit_counts`: the counts of one ctx shard add up to exactly 48, and the largest count of every ctx shard is 6.
All inputs are finite; a program needn't handle non-finite values.
Results may differ from a plain program's by a relative error of at most 0.022.
Values may be sent and summed in bfloat16 or wider, within the bound.
No kernel may reach another device: no remote copies, remote signals or barrier semaphores. Data moves between devices by JAX's collectives and lax.ppermute only.
A program may use at most 64 MiB of HBM per device.

v0:
```python
import jax
import jax.numpy as jnp
from jax import lax
from jax.sharding import PartitionSpec as P


def body(
    tokens,
    shared_gate,
    shared_up,
    shared_down,
    expert_gate,
    expert_up,
    expert_down,
    hit_rows,
    hit_counts,
    hit_weights,
):
    whole = lax.all_gather(tokens, "exp", axis=1, tiled=True)
    owner = lax.axis_index("exp")
    gate_sum = jnp.dot(
        whole,
        lax.all_gather(shared_gate, "ctx", axis=0, tiled=True),
        preferred_element_type=jnp.float32,
    )
    up_sum = jnp.dot(
        whole,
        lax.all_gather(shared_up, "ctx", axis=0, tiled=True),
        preferred_element_type=jnp.float32,
    )
    shared_hidden = (jax.nn.silu(gate_sum) * up_sum).astype(jnp.bfloat16)
    own_rows = hit_rows[0]
    capacity = own_rows.shape[1]
    slot_ids = jnp.arange(capacity, dtype=jnp.int32)
    live = slot_ids[None, :] < hit_counts[0][:, None]
    weights_all = jnp.where(live, hit_weights[0], 0.0)
    my_rows = lax.dynamic_index_in_dim(own_rows, owner, 0, keepdims=False)
    my_weights = lax.dynamic_index_in_dim(weights_all, owner, 0, keepdims=False)
    picked = whole[my_rows]
    arrived = lax.all_to_all(picked, "ctx", split_axis=1, concat_axis=0, tiled=True)
    gate_part = jnp.dot(arrived, expert_gate[0], preferred_element_type=jnp.float32)
    up_part = jnp.dot(arrived, expert_up[0], preferred_element_type=jnp.float32)
    gate_full, up_full = (
        lax.psum(gate_part.astype(jnp.bfloat16), "ctx").astype(jnp.float32),
        lax.psum(up_part.astype(jnp.bfloat16), "ctx").astype(jnp.float32),
    )
    hidden = (jax.nn.silu(gate_full) * up_full).astype(jnp.bfloat16)
    output = jnp.dot(hidden, expert_down[0], preferred_element_type=jnp.float32)
    returned = lax.all_to_all(
        output.astype(jnp.bfloat16), "ctx", split_axis=0, concat_axis=1, tiled=True
    ).astype(output.dtype)
    weighted = returned * my_weights[:, None]
    block_rows = lax.all_to_all(shared_down, "exp", split_axis=0, concat_axis=1, tiled=True)
    shared_part = jnp.dot(shared_hidden, block_rows, preferred_element_type=jnp.float32)
    partial_value = shared_part.at[my_rows].add(weighted)
    return lax.psum_scatter(
        partial_value.astype(jnp.bfloat16), "exp", scatter_dimension=1, tiled=True
    )


def solution(mesh):
    placed = (
        P("ctx", "exp"),
        P("ctx", "exp"),
        P("ctx", "exp"),
        P(None, "exp"),
        P("exp", "ctx", None),
        P("exp", "ctx", None),
        P("exp", None, "ctx"),
        P("ctx", None, None),
        P("ctx", None),
        P("ctx", None, None),
    )
    return jax.shard_map(
        body, mesh=mesh, in_specs=placed, out_specs=P("ctx", "exp"), check_vma=False
    )
```

profile of v0, /device:TPU:1, one launch (start us, length us, event | category | flops | bytes accessed | tf_op | source)
XLA Modules:
  0.0 854.5 jit_solution(12070856794549475238)
XLA Ops:
  6.5 0.0 copy-start
  6.5 0.0 all-gather.4.cloned.1.call-start
  6.5 0.7 all-gather.4.cloned.1.call-update
  7.3 0.0 all-gather.6.cloned.1.call-start
  7.3 0.7 all-gather.6.cloned.1.call-update
  8.0 0.0 all-reduce.3.cloned.1.call-start
  8.1 1.0 dynamic-slice_reduce_fusion.1
  9.0 130.8 %all-gather.4.cloned.1.call-done = bf16[256,7168]{0,1:T(8,128)(2,1)} async-done(((bf16[256,448]{0,1:T(8,128)(2,1)}), bf16[256,7168]{0,1:T(8,128)(2,1)}) %all-gather.4.cloned.1.call-update) | async-done | bytes 3670032 | tf_op jit(solution)/shard_map/all_gather | solution.py:19
  139.9 6.0 copy.24
  145.8 0.0 copy-start.1
  145.8 3.3 gather_fusion
  149.1 0.2 all_to_all.42
  149.3 0.1 copy.25
  149.3 18.1 %all_to_all.51 = bf16[6,32,224]{2,0,1:T(8,128)(2,1)S(1)} all-to-all(bf16[6,32,224]{2,0,1:T(8,128)(2,1)S(1)} %copy.25), channel_id=1, replica_groups=mesh['ctx'=32,'exp'=16] {'ctx'}, dimensions={1} | all-to-all | bytes 172032 | tf_op jit(solution)/shard_map/all_to_all | solution.py:40
  167.5 0.1 all_to_all.45
  167.5 0.0 copy-done.1
  167.5 0.0 copy-start.2
  167.6 1.2 convolution_convert_fusion
  168.8 0.0 copy-done.2
  168.8 1.3 convolution_convert_fusion.1
  170.1 0.0 all-reduce.3.cloned.1.call-update
  170.1 0.0 all-gather.8.cloned.1.call-start
  170.1 0.5 all-gather.8.cloned.1.call-update
  170.7 0.0 copy-done
  170.7 1.7 copy_bitcast_fusion
  172.4 0.0 copy-start.3
  172.4 4.8 all-to-all-start
  177.2 0.0 copy-done.3
  177.2 0.0 copy-done.4
  177.3 0.2 dynamic-slice_reduce_fusion
  177.5 39.5 %all-gather.6.cloned.1.call-done = bf16[7168,128]{1,0:T(8,128)(2,1)} async-done(((bf16[224,128]{1,0:T(8,128)(2,1)}), bf16[7168,128]{1,0:T(8,128)(2,1)}) %all-gather.6.cloned.1.call-update) | async-done | bytes 1835024 | tf_op jit(solution)/shard_map/all_gather | solution.py:23
  217.0 3.8 fusion.23
  220.7 302.7 %all-reduce.3.cloned.1.call-done = (bf16[192,2048]{1,0:T(8,128)(2,1)}, bf16[192,2048]{1,0:T(8,128)(2,1)}) async-done(((bf16[192,2048]{1,0:T(8,128)(2,1)}, bf16[192,2048]{1,0:T(8,128)(2,1)}), (bf16[192,2048]{1,0:T(8,128)(2,1)}, bf16[192,2048]{1,0:T(8,128)(2,1)})) %all-reduce.3.cloned.1.call-update) | async-done | bytes 1572880 | tf_op jit(solution)/shard_map/psum | solution.py:45
  523.4 2.3 convolution_convert_fusion.2
  525.7 0.7 all_to_all.46
  526.4 0.0 all-to-all-done
  526.4 7.7 all-to-all-start.2
  534.1 0.0 reduce-scatter.4.cloned.1.call-start
  534.2 53.4 %all-gather.8.cloned.1.call-done = bf16[7168,128]{1,0:T(8,128)(2,1)} async-done(((bf16[224,128]{1,0:T(8,128)(2,1)}), bf16[7168,128]{1,0:T(8,128)(2,1)}) %all-gather.8.cloned.1.call-update) | async-done | bytes 1835024 | tf_op jit(solution)/shard_map/all_gather | solution.py:28
  587.6 8.3 fusion.6
  595.9 0.0 all-to-all-done.2
  595.9 0.1 copy.26
  596.0 0.2 reshape.44
  596.1 6.8 scatter_custom_fusion
  603.0 5.5 convert_element_type.43
  608.5 5.9 copy.28
  614.4 0.0 reduce-scatter.4.cloned.1.call-update
  614.4 233.5 %reduce-scatter.4.cloned.1.call-done = bf16[448,256]{1,0:T(8,128)(2,1)} async-done(((bf16[7168,256]{1,0:T(8,128)(2,1)}), bf16[448,256]{1,0:T(8,128)(2,1)}) %reduce-scatter.4.cloned.1.call-update) | async-done | bytes 229392
  (5 shorter events, 0.0 us)
Async XLA Ops:
  6.5 164.1 %copy-start = (bf16[2048,448]{0,1:T(8,128)(2,1)S(1)}, bf16[2048,448]{0,1:T(8,128)(2,1)}, u32[]{:S(2)}) copy-start(bf16[2048,448]{0,1:T(8,128)(2,1)} %param.13) | copy-start | bytes 5505028
  6.5 133.3 %all-gather.4.cloned.1.call-start = ((), (), s32[]{:S(2)}) async-start(), calls=%async_computation.4 | async-start | bytes 3899392 | tf_op jit(solution)/shard_map/all_gather | solution.py:19
  7.3 209.7 %all-gather.6.cloned.1.call-start = ((), (), s32[]{:S(2)}) async-start(), calls=%async_computation.5 | async-start | bytes 1892352 | tf_op jit(solution)/shard_map/all_gather | solution.py:23
  8.0 515.4 %all-reduce.3.cloned.1.call-start = ((), (), s32[]{:S(2)}) async-start(), calls=%async_computation.8 | async-start | bytes 3145728 | tf_op jit(solution)/shard_map/psum | solution.py:45
  145.8 21.7 %copy-start.1 = (bf16[1,224,2048]{2,1,0:T(8,128)(2,1)S(1)}, bf16[1,224,2048]{2,1,0:T(8,128)(2,1)}, u32[]{:S(2)}) copy-start(bf16[1,224,2048]{2,1,0:T(8,128)(2,1)} %param.15) | copy-start | bytes 2752516
  167.5 1.2 copy-start.2
  170.1 417.5 %all-gather.8.cloned.1.call-start = ((), (), s32[]{:S(2)}) async-start(), calls=%async_computation.6 | async-start | bytes 1892352 | tf_op jit(solution)/shard_map/all_gather | solution.py:28
  172.4 4.9 copy-start.3
  172.4 4.9 copy-start.4
  172.4 354.0 %all-to-all-start = ((bf16[16,128,448]{1,2,0:T(8,128)(2,1)}), bf16[16,128,448]{1,2,0:T(8,128)(2,1)}, u32[]{:S(2)}, u32[]{:S(2)}) async-start(bf16[16,128,448]{1,2,0:T(8,128)(2,1)} %copy_bitcast_fusion), calls=%async_computation | async-start | bytes 3670016 | tf_op jit(solution)/shard_map/all_to_all | solution.py:53
  526.4 69.5 %all-to-all-start.2 = ((bf16[32,6,224]{2,1,0:T(8,128)(2,1)}), bf16[32,6,224]{2,1,0:T(8,128)(2,1)S(1)}, u32[]{:S(2)}, u32[]{:S(2)}) async-start(bf16[32,6,224]{2,1,0:T(8,128)(2,1)} %all_to_all.46), calls=%async_computation.2 | async-start | bytes 262144 | tf_op jit(solution)/shard_map/all_to_all | solution.py:49
  534.1 313.8 %reduce-scatter.4.cloned.1.call-start = ((), (), s32[]{:S(2)}) async-start(), calls=%async_computation.7 | async-start | bytes 3899392
Sparse Core Ops, SparseCore 0:
  10.5 129.2 all-gather.3
  142.0 74.8 all-gather.5
  219.9 303.4 all-reduce.2
  525.6 61.9 all-gather.7
  614.6 233.3 reduce-scatter.3
where the time goes:
time: 858 us; the launch traced here: 854 us
  waiting for transfers between devices  762 us (89%)
  local copies, waits for them, and re-layouts  19.3 us (2%)
  blocking collectives  18.1 us (2%)
  matrix products  16.8 us (2%)
  between operations  13.3 us (2%)
  starting transfers between devices  12.7 us (1%)
  other arithmetic  12.4 us (1%)
    psum x1, waiting for transfers between devices, body(): lax.psum(up_part.astype(jnp.bfloat16), 'ctx').astype(jnp.float32)  303 us
    unnamed x6, waiting for transfers between devices  235 us
    all_gather x1, waiting for transfers between devices, body(): whole = lax.all_gather(tokens, 'exp', axis=1, tiled=True)  131 us
    all_gather x1, waiting for transfers between devices, body(): lax.all_gather(shared_up, 'ctx', axis=0, tiled=True)  53.4 us
    all_gather x1, waiting for transfers between devices, body(): lax.all_gather(shared_gate, 'ctx', axis=0, tiled=True)  39.5 us
    all_to_all x1, blocking collectives, body(): lax.all_to_all(picked, 'ctx', split_axis=1, concat_axis=0, tiled=True)  18.1 us
  transfers between devices with their start and end apart: 7, of which 5 were waited for; matrix products, arithmetic and copies ran while one was open for 3% of the time, Pallas kernels for 0%

commit v1 on v0

v1 whole, which is shorter than its diff:
```python
import jax
import jax.numpy as jnp
from jax import lax
from jax.experimental import pallas as pl
from jax.experimental.pallas import tpu as pltpu
from jax.sharding import Mesh, PartitionSpec as P

CTX = ("z", "x", "c")
CHIP = ("z", "x")
EXP = ("y", "h")
f32, bf16 = jnp.float32, jnp.bfloat16


def exchange(v, axes):
    return lax.all_to_all(v, axes, 0, 0, tiled=True)


def gather(v, axes, n):
    return exchange(jnp.broadcast_to(v[None], (n,) + v.shape), axes)


def swap(v, axis):
    return lax.ppermute(v, axis, [(0, 1), (1, 0)])


def dot(a, b):
    return jnp.dot(a, b, preferred_element_type=f32)


def in_kernel(tok, own, other, out):
    for f in range(2):
        acc = jnp.zeros((256, 256), f32)
        for z in range(4):
            for a in range(2):
                w = jnp.concatenate([own[2 * a + f, z], other[2 * a + f, z]], axis=0)
                acc += dot(tok[2 * z + a], w)
        out[:, f * 256:(f + 1) * 256] = acc


def out_kernel(hid, down, spread, slots, out):
    acc = dot(spread[...], slots[...])
    for y in range(8):
        acc += dot(hid[y], down[y])
    out[...] = acc.astype(bf16)


def body(tokens, shared_gate, shared_up, shared_down, expert_gate, expert_up,
         expert_down, hit_rows, hit_counts, hit_weights):
    core = lax.axis_index("c")
    half = lax.axis_index("h")
    expert = lax.axis_index(EXP)
    first = core == 0

    ids = hit_rows[0].reshape(96)
    pick = (ids[:, None] == jnp.arange(256, dtype=jnp.int32)[None, :]).astype(bf16)
    picked = dot(pick, tokens).astype(bf16).reshape(16, 6, 448)
    mine = exchange(picked, EXP)
    both = jnp.stack([mine, jnp.roll(mine, 224, axis=-1)], axis=1).reshape(32, 6, 448)
    arrived = exchange(both, CTX).reshape(192, 448)

    def halves(w, axis):
        lo, hi = jnp.split(w, 2, axis=axis)
        return jnp.where(first, lo, hi), jnp.where(first, hi, lo)

    g_own, g_send = halves(expert_gate[0], 1)
    u_own, u_send = halves(expert_up[0], 1)
    d_own, d_send = halves(expert_down[0], 0)
    g_w = jnp.concatenate([g_own, swap(g_send, "c")], axis=0)
    u_w = jnp.concatenate([u_own, swap(u_send, "c")], axis=0)
    d_other = swap(d_send, "c")

    g_part = dot(arrived, g_w).astype(bf16).reshape(16, 12, 1024)
    u_part = dot(arrived, u_w).astype(bf16).reshape(16, 12, 1024)
    sums = exchange(jnp.concatenate([g_part, u_part], axis=1), CHIP)
    sums = jnp.sum(sums.astype(f32), axis=0)
    hidden = (jax.nn.silu(sums[:12]) * sums[12:]).astype(bf16)
    hidden = gather(hidden, CHIP, 16).reshape(192, 1024)
    o_own, o_other = dot(hidden, d_own), dot(hidden, d_other)
    o_part = jnp.concatenate(
        [jnp.where(first, o_own, o_other), jnp.where(first, o_other, o_own)], axis=1)
    back = exchange(o_part.astype(bf16).reshape(32, 6, 448), CTX)
    back = jnp.sum(back.astype(f32).reshape(16, 2, 6, 448), axis=1)
    live = jnp.arange(6, dtype=jnp.int32)[None, :] < hit_counts[0][:, None]
    weights = jnp.where(live, hit_weights[0], 0.0)
    weight = lax.dynamic_index_in_dim(weights, expert, 0, keepdims=False)
    back = (back * weight[None, :, None]).astype(bf16)
    slots = exchange(back, EXP).reshape(96, 448)

    tok = jnp.where(first, tokens, jnp.roll(tokens, 224, axis=1))
    tok = gather(tok, "y", 8)
    w = jnp.concatenate([shared_gate, shared_up], axis=1)
    turn = []
    for x in range(4):
        for h in range(2):
            turn.append((2 * x + h, 2 * ((x & 2) | h) + (x & 1)))
    w = lax.ppermute(w, ("x", "h"), turn)
    w = gather(w, "z", 4)
    w = gather(w, "x", 4)
    w_other = swap(w, "c")
    part = pl.pallas_call(
        in_kernel, out_shape=jax.ShapeDtypeStruct((256, 512), f32),
        compiler_params=pltpu.CompilerParams(vmem_limit_bytes=40 << 20),
    )(tok, w, w_other)
    lo, hi = part[:128], part[128:]
    keep = jnp.where(half == 0, lo, hi)
    send = jnp.where(half == 0, hi, lo).astype(bf16)
    total = (keep + swap(send, "h").astype(f32)).reshape(128, 2, 2, 128)
    sh = (jax.nn.silu(total[:, :, 0]) * total[:, :, 1]).astype(bf16).reshape(128, 256)
    sh = gather(sh, EXP, 16).reshape(8, 256, 256)

    spread = (ids[None, :] == jnp.arange(256, dtype=jnp.int32)[:, None]).astype(bf16)
    return pl.pallas_call(
        out_kernel, out_shape=jax.ShapeDtypeStruct((256, 448), bf16),
        compiler_params=pltpu.CompilerParams(vmem_limit_bytes=40 << 20),
    )(sh, shared_down.reshape(8, 256, 448), spread, slots)


def solution(mesh):
    fine = Mesh(mesh.devices.reshape(4, 4, 2, 8, 2), ("z", "x", "c", "y", "h"))
    placed = (
        P(CTX, EXP),
        P(CTX, EXP),
        P(CTX, EXP),
        P(None, EXP),
        P(EXP, CTX, None),
        P(EXP, CTX, None),
        P(EXP, None, CTX),
        P(CTX, None, None),
        P(CTX, None),
        P(CTX, None, None),
    )
    return jax.shard_map(
        body, mesh=fine, in_specs=placed, out_specs=P(CTX, EXP), check_vma=False)
```

time: 858 us -> 292 us (0.34)
  the two profiles are of different devices: /device:TPU:1 before, /device:TPU:32 now
where the time goes in v1:
time: 292 us; the launch traced here: 291 us
  waiting for transfers between devices  159 us (54%)
  starting transfers between devices  82.7 us (28%)
  blocking collectives  19.3 us (7%)
  local copies, waits for them, and re-layouts  16.1 us (6%)
  other arithmetic  5.31 us (2%)
  matrix products  4.55 us (2%)
  Pallas kernels  4.05 us (1%)
    all_to_all x9, waiting for transfers between devices, exchange(): return lax.all_to_all(v, axes, 0, 0, tiled=True)  157 us
    all_to_all x9, starting transfers between devices, exchange(): return lax.all_to_all(v, axes, 0, 0, tiled=True)  72.1 us
    all_to_all x1, blocking collectives, exchange(): return lax.all_to_all(v, axes, 0, 0, tiled=True)  19.3 us
    ppermute x5, starting transfers between devices, swap(): return lax.ppermute(v, axis, [(0, 1), (1, 0)])  9.86 us
  transfers between devices with their start and end apart: 15, of which 10 were waited for; matrix products, arithmetic and copies ran while one was open for 5% of the time, Pallas kernels for 0%

profile of v1, /device:TPU:32, one launch (start us, length us, event | category | flops | bytes accessed | tf_op | source)
XLA Modules:
  0.0 291.1 jit_solution(8342043920578590690)
XLA Ops:
  0.0 0.8 copy.23
  0.8 1.2 convolution_convert_fusion.2
  2.0 0.7 reshape.76
  2.7 15.7 %all-to-all-start.4 = ((bf16[16,6,448]{2,1,0:T(8,128)(2,1)}), bf16[16,6,448]{2,1,0:T(8,128)(2,1)S(1)}, u32[]{:S(2)}, u32[]{:S(2)}) async-start(bf16[16,6,448]{2,1,0:T(8,128)(2,1)} %reshape.76), calls=%async_computation.4 | async-start | bytes 262144 | tf_op jit(solution)/shard_map/all_to_all | solution.py:15
  18.4 1.3 broadcast_select_fusion.1
  19.7 1.9 collective-permute-start.4
  21.6 5.6 %all-to-all-done.4 = bf16[16,6,448]{2,1,0:T(8,128)(2,1)S(1)} async-done(((bf16[16,6,448]{2,1,0:T(8,128)(2,1)}), bf16[16,6,448]{2,1,0:T(8,128)(2,1)S(1)}, u32[]{:S(2)}, u32[]{:S(2)}) %all-to-all-start.4) | async-done | bytes 86048 | tf_op jit(solution)/shard_map/all_to_all | solution.py:15
  27.5 0.7 copy.27
  28.2 7.1 %all-to-all-start.5 = ((bf16[32,6,448]{2,1,0:T(8,128)(2,1)}), bf16[32,6,448]{2,1,0:T(8,128)(2,1)S(1)}, u32[]{:S(2)}, u32[]{:S(2)}) async-start(bf16[32,6,448]{2,1,0:T(8,128)(2,1)} %bitcast.4), calls=%async_computation.5 | async-start | bytes 524288 | tf_op jit(solution)/shard_map/all_to_all | solution.py:15
  35.4 2.2 collective-permute-start.3
  37.6 8.8 %all-to-all-done.5 = bf16[32,6,448]{2,1,0:T(8,128)(2,1)S(1)} async-done(((bf16[32,6,448]{2,1,0:T(8,128)(2,1)}), bf16[32,6,448]{2,1,0:T(8,128)(2,1)S(1)}, u32[]{:S(2)}, u32[]{:S(2)}) %all-to-all-start.5) | async-done | bytes 172064 | tf_op jit(solution)/shard_map/all_to_all | solution.py:15
  46.6 1.4 convolution_convert_fusion
  48.1 1.4 convolution_convert_fusion.1
  49.6 1.1 pad_maximum_fusion
  50.7 3.6 %all-to-all-start.6 = ((bf16[16,24,1024]{2,1,0:T(8,128)(2,1)}), bf16[16,24,1024]{2,1,0:T(8,128)(2,1)S(1)}, u32[]{:S(2)}, u32[]{:S(2)}) async-start(bf16[16,24,1024]{2,1,0:T(8,128)(2,1)} %pad_maximum_fusion), calls=%async_computation.6 | async-start | bytes 1572864 | tf_op jit(solution)/shard_map/all_to_all | solution.py:15
  54.4 0.7 collective-permute-start
  55.1 22.0 %all-to-all-done.6 = bf16[16,24,1024]{2,1,0:T(8,128)(2,1)S(1)} async-done(((bf16[16,24,1024]{2,1,0:T(8,128)(2,1)}), bf16[16,24,1024]{2,1,0:T(8,128)(2,1)S(1)}, u32[]{:S(2)}, u32[]{:S(2)}) %all-to-all-start.6) | async-done | bytes 786464 | tf_op jit(solution)/shard_map/all_to_all | solution.py:15
  77.1 0.8 broadcast_in_dim.15
  77.9 4.6 %all-to-all-start.1 = ((bf16[4,224,256]{2,1,0:T(8,128)(2,1)}), bf16[4,224,256]{2,1,0:T(8,128)(2,1)S(1)}, u32[]{:S(2)}, u32[]{:S(2)}) async-start(bf16[4,224,256]{2,1,0:T(8,128)(2,1)} %broadcast_in_dim.15), calls=%async_computation.1 | async-start | bytes 917504 | tf_op jit(solution)/shard_map/all_to_all | solution.py:15
  82.6 12.4 %all-to-all-done.1 = bf16[4,224,256]{2,1,0:T(8,128)(2,1)S(1)} async-done(((bf16[4,224,256]{2,1,0:T(8,128)(2,1)}), bf16[4,224,256]{2,1,0:T(8,128)(2,1)S(1)}, u32[]{:S(2)}, u32[]{:S(2)}) %all-to-all-start.1) | async-done | bytes 458784 | tf_op jit(solution)/shard_map/all_to_all | solution.py:15
  95.0 19.3 %all_to_all.50 = bf16[16,12,1024]{2,1,0:T(8,128)(2,1)S(1)} all-to-all(bf16[16,12,1024]{2,1,0:T(8,128)(2,1)S(1)} %broadcast_in_dim.18), channel_id=1, replica_groups=mesh['z'=4,'x'=4,'c'=2,'y'=8,'h'=2] {'z','x'}, dimensions={0} | all-to-all | bytes 786432 | tf_op jit(solution)/shard_map/all_to_all | solution.py:15
  114.3 1.4 broadcast_in_dim.16
  115.7 4.5 %all-to-all-start.2 = ((bf16[4,4,224,256]{3,2,1,0:T(8,128)(2,1)}), bf16[4,4,224,256]{3,2,1,0:T(8,128)(2,1)}, u32[]{:S(2)}, u32[]{:S(2)}) async-start(bf16[4,4,224,256]{3,2,1,0:T(8,128)(2,1)} %broadcast_in_dim.16), calls=%async_computation.2 | async-start | bytes 3670016 | tf_op jit(solution)/shard_map/all_to_all | solution.py:15
  120.3 1.9 collective-permute-start.5
  122.7 1.4 collective-permute-done.5
  124.4 0.8 pad_maximum_fusion.2
  125.2 16.6 %all-to-all-done.2.own = bf16[4,4,224,256]{3,2,1,0:T(8,128)(2,1)} async-done(((bf16[4,4,224,256]{3,2,1,0:T(8,128)(2,1)}), bf16[4,4,224,256]{3,2,1,0:T(8,128)(2,1)}, u32[]{:S(2)}, u32[]{:S(2)}) %all-to-all-start.2) | async-done | bytes 1835040 | tf_op jit(solution)/shard_map/all_to_all | solution.py:15
  141.8 5.9 %all-to-all-start.8 = ((bf16[32,6,448]{2,1,0:T(8,128)(2,1)}), bf16[32,6,448]{2,1,0:T(8,128)(2,1)S(1)}, u32[]{:S(2)}, u32[]{:S(2)}) async-start(bf16[32,6,448]{2,1,0:T(8,128)(2,1)} %pad_maximum_fusion.2), calls=%async_computation.8 | async-start | bytes 524288 | tf_op jit(solution)/shard_map/all_to_all | solution.py:15
  147.9 11.0 %all-to-all-done.8 = bf16[32,6,448]{2,1,0:T(8,128)(2,1)S(1)} async-done(((bf16[32,6,448]{2,1,0:T(8,128)(2,1)}), bf16[32,6,448]{2,1,0:T(8,128)(2,1)S(1)}, u32[]{:S(2)}, u32[]{:S(2)}) %all-to-all-start.8) | async-done | bytes 172064 | tf_op jit(solution)/shard_map/all_to_all | solution.py:15
  158.9 1.4 broadcast_in_dim.14
  160.2 9.4 %all-to-all-start = ((bf16[8,256,448]{1,2,0:T(8,128)(2,1)}), bf16[8,256,448]{1,2,0:T(8,128)(2,1)}, u32[]{:S(2)}, u32[]{:S(2)}) async-start(bf16[8,256,448]{1,2,0:T(8,128)(2,1)} %broadcast_in_dim.14), calls=%async_computation | async-start | bytes 3670016 | tf_op jit(solution)/shard_map/all_to_all | solution.py:15
  169.7 1.9 collective-permute-start.1
  171.9 38.8 %all-to-all-done = bf16[8,256,448]{1,2,0:T(8,128)(2,1)} async-done(((bf16[8,256,448]{1,2,0:T(8,128)(2,1)}), bf16[8,256,448]{1,2,0:T(8,128)(2,1)}, u32[]{:S(2)}, u32[]{:S(2)}) %all-to-all-start) | async-done | bytes 1835040 | tf_op jit(solution)/shard_map/all_to_all | solution.py:15
  210.7 2.8 copy.21.tok
  213.5 3.3 %shard_map.100 = f32[256,512]{1,0:T(8,128)S(1)} custom-call(bf16[8,256,448]{2,1,0:T(8,128)(2,1)S(1)} %copy.21.tok, bf16[4,4,224,256]{3,2,1,0:T(8,128)(2,1)} %all-to-all-done.2.own, bf16[4,4,224,256]{3,2,1,0:T(8,128)(2,1)} %collective-permute-done.1.other), custom_call_target="tpu_custom_call" | custom-call | tf_op jit(solution)/shard_map/pallas_call | solution.py:100
  216.9 1.9 collective-permute-start.2
  218.8 0.7 multiply_convert_fusion
  219.5 12.7 %all-to-all-start.9 = ((bf16[16,6,448]{2,1,0:T(8,128)(2,1)}), bf16[16,6,448]{2,1,0:T(8,128)(2,1)S(1)}, u32[]{:S(2)}, u32[]{:S(2)}) async-start(bf16[16,6,448]{2,1,0:T(8,128)(2,1)} %multiply_convert_fusion), calls=%async_computation.9 | async-start | bytes 262144 | tf_op jit(solution)/shard_map/all_to_all | solution.py:15
  232.5 0.8 slice_reduce_fusion.1
  233.3 7.4 %all-to-all-done.9 = bf16[16,6,448]{2,1,0:T(8,128)(2,1)S(1)} async-done(((bf16[16,6,448]{2,1,0:T(8,128)(2,1)}), bf16[16,6,448]{2,1,0:T(8,128)(2,1)S(1)}, u32[]{:S(2)}, u32[]{:S(2)}) %all-to-all-start.9) | async-done | bytes 86048 | tf_op jit(solution)/shard_map/all_to_all | solution.py:15
  240.7 1.1 broadcast_in_dim.17
  241.8 8.6 %all-to-all-start.3 = ((bf16[16,128,256]{2,1,0:T(8,128)(2,1)}), bf16[16,128,256]{2,1,0:T(8,128)(2,1)S(1)}, u32[]{:S(2)}, u32[]{:S(2)}) async-start(bf16[16,128,256]{2,1,0:T(8,128)(2,1)} %broadcast_in_dim.17), calls=%async_computation.3 | async-start | bytes 2097152 | tf_op jit(solution)/shard_map/all_to_all | solution.py:15
  250.4 2.8 copy.22
  253.2 0.7 fusion.16.spread
  254.0 34.7 %all-to-all-done.3 = bf16[16,128,256]{2,1,0:T(8,128)(2,1)S(1)} async-done(((bf16[16,128,256]{2,1,0:T(8,128)(2,1)}), bf16[16,128,256]{2,1,0:T(8,128)(2,1)S(1)}, u32[]{:S(2)}, u32[]{:S(2)}) %all-to-all-start.3) | async-done | bytes 1048608 | tf_op jit(solution)/shard_map/all_to_all | solution.py:15
  288.7 0.8 copy-done
  289.5 0.8 shard_map.101
  290.3 0.8 copy.26
  (48 shorter events, 2.5 us)
Async XLA Ops:
  2.7 24.5 %all-to-all-start.4 = ((bf16[16,6,448]{2,1,0:T(8,128)(2,1)}), bf16[16,6,448]{2,1,0:T(8,128)(2,1)S(1)}, u32[]{:S(2)}, u32[]{:S(2)}) async-start(bf16[16,6,448]{2,1,0:T(8,128)(2,1)} %reshape.76), calls=%async_computation.4 | async-start | bytes 262144 | tf_op jit(solution)/shard_map/all_to_all | solution.py:15
  18.4 17.0 %copy-start.3 = (bf16[1,224,2048]{2,1,0:T(8,128)(2,1)S(1)}, bf16[1,224,2048]{2,1,0:T(8,128)(2,1)}, u32[]{:S(2)}) copy-start(bf16[1,224,2048]{2,1,0:T(8,128)(2,1)} %param.14) | copy-start | bytes 2752516
  19.7 26.9 %collective-permute-start.4 = (bf16[224,1024]{1,0:T(8,128)(2,1)S(1)}, bf16[224,1024]{1,0:T(8,128)(2,1)}, u32[]{:S(2)}, u32[]{:S(2)}) collective-permute-start(bf16[224,1024]{1,0:T(8,128)(2,1)S(1)} %get-tuple-element.10), channel_id=1, source_target_pairs={{0,16},{16,0},{1,17},{17,1},{2,18},{18,2},{3,19},{19,3},{4,20},{20... | collective-permute-start | bytes 1376264 | tf_op jit(solution)/shard_map/ppermute | solution.py:23
  28.2 18.2 %all-to-all-start.5 = ((bf16[32,6,448]{2,1,0:T(8,128)(2,1)}), bf16[32,6,448]{2,1,0:T(8,128)(2,1)S(1)}, u32[]{:S(2)}, u32[]{:S(2)}) async-start(bf16[32,6,448]{2,1,0:T(8,128)(2,1)} %bitcast.4), calls=%async_computation.5 | async-start | bytes 524288 | tf_op jit(solution)/shard_map/all_to_all | solution.py:15
  35.4 12.7 %collective-permute-start.3 = (bf16[224,1024]{1,0:T(8,128)(2,1)S(1)}, bf16[224,1024]{1,0:T(8,128)(2,1)}, u32[]{:S(2)}, u32[]{:S(2)}) collective-permute-start(bf16[224,1024]{1,0:T(8,128)(2,1)S(1)} %get-tuple-element.8), channel_id=1, source_target_pairs={{0,16},{16,0},{1,17},{17,1},{2,18},{18,2},{3,19},{19,3},{4,20},{20... | collective-permute-start | bytes 1376264 | tf_op jit(solution)/shard_map/ppermute | solution.py:23
  49.6 4.8 %copy-start.4 = (bf16[224,128]{1,0:T(8,128)(2,1)S(1)}, bf16[224,128]{1,0:T(8,128)(2,1)}, u32[]{:S(2)}) copy-start(bf16[224,128]{1,0:T(8,128)(2,1)} %param.12) | copy-start | bytes 172036
  49.6 4.8 %copy-start.5 = (bf16[224,128]{1,0:T(8,128)(2,1)S(1)}, bf16[224,128]{1,0:T(8,128)(2,1)}, u32[]{:S(2)}) copy-start(bf16[224,128]{1,0:T(8,128)(2,1)} %param.11) | copy-start | bytes 172036
  50.7 26.4 %all-to-all-start.6 = ((bf16[16,24,1024]{2,1,0:T(8,128)(2,1)}), bf16[16,24,1024]{2,1,0:T(8,128)(2,1)S(1)}, u32[]{:S(2)}, u32[]{:S(2)}) async-start(bf16[16,24,1024]{2,1,0:T(8,128)(2,1)} %pad_maximum_fusion), calls=%async_computation.6 | async-start | bytes 1572864 | tf_op jit(solution)/shard_map/all_to_all | solution.py:15
  54.4 0.7 collective-permute-start
  77.9 17.1 %all-to-all-start.1 = ((bf16[4,224,256]{2,1,0:T(8,128)(2,1)}), bf16[4,224,256]{2,1,0:T(8,128)(2,1)S(1)}, u32[]{:S(2)}, u32[]{:S(2)}) async-start(bf16[4,224,256]{2,1,0:T(8,128)(2,1)} %broadcast_in_dim.15), calls=%async_computation.1 | async-start | bytes 917504 | tf_op jit(solution)/shard_map/all_to_all | solution.py:15
  115.7 4.5 %copy-start.2 = (bf16[1,2048,224]{1,2,0:T(8,128)(2,1)S(1)}, bf16[1,2048,224]{1,2,0:T(8,128)(2,1)}, u32[]{:S(2)}) copy-start(bf16[1,2048,224]{1,2,0:T(8,128)(2,1)} %param.16) | copy-start | bytes 2752516
  115.7 26.1 %all-to-all-start.2 = ((bf16[4,4,224,256]{3,2,1,0:T(8,128)(2,1)}), bf16[4,4,224,256]{3,2,1,0:T(8,128)(2,1)}, u32[]{:S(2)}, u32[]{:S(2)}) async-start(bf16[4,4,224,256]{3,2,1,0:T(8,128)(2,1)} %broadcast_in_dim.16), calls=%async_computation.2 | async-start | bytes 3670016 | tf_op jit(solution)/shard_map/all_to_all | solution.py:15
  120.3 3.7 %collective-permute-start.5 = (bf16[1024,224]{0,1:T(8,128)(2,1)S(1)}, bf16[1024,224]{0,1:T(8,128)(2,1)S(1)}, u32[]{:S(2)}, u32[]{:S(2)}) collective-permute-start(bf16[1024,224]{0,1:T(8,128)(2,1)S(1)} %select_bitcast_fusion), channel_id=1, source_target_pairs={{0,16},{16,0},{1,17},{17,1},{2,18},{18,2},{3,19},{19,3},{4,20},{20... | collective-permute-start | bytes 1376264 | tf_op jit(solution)/shard_map/ppermute | solution.py:23
  122.3 25.4 %copy-start.1 = (bf16[256,448]{0,1:T(8,128)(2,1)S(1)}, bf16[256,448]{0,1:T(8,128)(2,1)}, u32[]{:S(2)}) copy-start(bf16[256,448]{0,1:T(8,128)(2,1)} %param.10) | copy-start | bytes 688132
  141.8 17.0 %all-to-all-start.8 = ((bf16[32,6,448]{2,1,0:T(8,128)(2,1)}), bf16[32,6,448]{2,1,0:T(8,128)(2,1)S(1)}, u32[]{:S(2)}, u32[]{:S(2)}) async-start(bf16[32,6,448]{2,1,0:T(8,128)(2,1)} %pad_maximum_fusion.2), calls=%async_computation.8 | async-start | bytes 524288 | tf_op jit(solution)/shard_map/all_to_all | solution.py:15
  160.2 11.4 %copy-start.6 = (f32[1,16,6]{1,0,2:T(1,128)S(1)}, f32[1,16,6]{1,0,2:T(1,128)}, u32[]{:S(2)}) copy-start(f32[1,16,6]{1,0,2:T(1,128)} %param.19) | copy-start | bytes 1156
  160.2 11.4 %copy-start.7 = (s32[1,16]{1,0:T(1,128)S(1)}, s32[1,16]{1,0:T(1,128)}, u32[]{:S(2)}) copy-start(s32[1,16]{1,0:T(1,128)} %param.18) | copy-start | bytes 196
  160.2 50.5 %all-to-all-start = ((bf16[8,256,448]{1,2,0:T(8,128)(2,1)}), bf16[8,256,448]{1,2,0:T(8,128)(2,1)}, u32[]{:S(2)}, u32[]{:S(2)}) async-start(bf16[8,256,448]{1,2,0:T(8,128)(2,1)} %broadcast_in_dim.14), calls=%async_computation | async-start | bytes 3670016 | tf_op jit(solution)/shard_map/all_to_all | solution.py:15
  169.7 43.8 %collective-permute-start.1 = (bf16[4,4,224,256]{3,2,1,0:T(8,128)(2,1)}, bf16[4,4,224,256]{3,2,1,0:T(8,128)(2,1)}, u32[]{:S(2)}, u32[]{:S(2)}) collective-permute-start(bf16[4,4,224,256]{3,2,1,0:T(8,128)(2,1)} %all-to-all-done.2.own), channel_id=1, source_target_pairs={{0,16},{16,0},{1,17},{17,1},{2,18},{18,2},{3,19},{19,3},{4,20},{20... | collective-permute-start | bytes 5505032 | tf_op jit(solution)/shard_map/ppermute | solution.py:23
  216.9 15.4 %collective-permute-start.2 = (bf16[128,512]{1,0:T(8,128)(2,1)S(1)}, bf16[128,512]{1,0:T(8,128)(2,1)S(1)}, u32[]{:S(2)}, u32[]{:S(2)}) collective-permute-start(bf16[128,512]{1,0:T(8,128)(2,1)S(1)} %select_convert_fusion), channel_id=1, source_target_pairs={{0,1},{1,0},{2,3},{3,2},{4,5},{5,4},{6,7},{7,6},{8,9},{9,8},{10,11... | collective-permute-start | bytes 393224 | tf_op jit(solution)/shard_map/ppermute | solution.py:23
  219.5 21.2 %all-to-all-start.9 = ((bf16[16,6,448]{2,1,0:T(8,128)(2,1)}), bf16[16,6,448]{2,1,0:T(8,128)(2,1)S(1)}, u32[]{:S(2)}, u32[]{:S(2)}) async-start(bf16[16,6,448]{2,1,0:T(8,128)(2,1)} %multiply_convert_fusion), calls=%async_computation.9 | async-start | bytes 262144 | tf_op jit(solution)/shard_map/all_to_all | solution.py:15
  241.8 46.9 %all-to-all-start.3 = ((bf16[16,128,256]{2,1,0:T(8,128)(2,1)}), bf16[16,128,256]{2,1,0:T(8,128)(2,1)S(1)}, u32[]{:S(2)}, u32[]{:S(2)}) async-start(bf16[16,128,256]{2,1,0:T(8,128)(2,1)} %broadcast_in_dim.17), calls=%async_computation.3 | async-start | bytes 2097152 | tf_op jit(solution)/shard_map/all_to_all | solution.py:15
  288.7 0.8 copy-start

commit v2 on v1

v2 whole, which is shorter than its diff:
```python
import jax
import jax.numpy as jnp
from jax import lax
from jax.experimental import pallas as pl
from jax.experimental.pallas import tpu as pltpu
from jax.sharding import Mesh, PartitionSpec as P

CTX = ("z", "x", "c")
CHIP = ("z", "x")
EXP = ("y", "h")
f32, bf16 = jnp.float32, jnp.bfloat16
VMEM = pltpu.CompilerParams(vmem_limit_bytes=40 << 20)


def exchange(v, axes):
    return lax.all_to_all(v, axes, 0, 0, tiled=True)


def gather(v, axes, n):
    return exchange(jnp.broadcast_to(v[None], (n,) + v.shape), axes)


def swap(v, axis):
    return lax.ppermute(v, axis, [(0, 1), (1, 0)])


def dot(a, b):
    return jnp.dot(a, b, preferred_element_type=f32)


def dot_t(a, b):
    return lax.dot_general(a, b, (((1,), (1,)), ((), ())), preferred_element_type=f32)


def call(kernel, shapes, *args, scalars=0, after=()):
    specs = [pl.BlockSpec(memory_space=pltpu.SMEM)] * scalars
    specs += [pl.BlockSpec(memory_space=pltpu.VMEM)] * (len(args) - scalars)
    specs += [pl.BlockSpec(memory_space=pl.ANY)] * len(after)
    count = len(args)

    def run(*refs):
        kernel(*refs[:count], *refs[count + len(after):])

    return pl.pallas_call(
        run, out_shape=[jax.ShapeDtypeStruct(*v) for v in shapes], in_specs=specs,
        compiler_params=VMEM)(*args, *after)


def stack_kernel(*refs):
    out = refs[-1]
    size = refs[0].shape[0]
    for i, ref in enumerate(refs[:-1]):
        out[i * size:(i + 1) * size] = ref[...]


def pick_kernel(spread, tokens_t, out):
    out[...] = dot_t(spread[...], tokens_t[...]).astype(bf16)


def double_kernel(rows, out):
    out[:, 0] = rows[...]
    out[:, 1] = rows[...]


def expert_kernel(rows, gate, up, out):
    to = lax.broadcasted_iota(jnp.int32, (384, 256), 0)
    at = lax.broadcasted_iota(jnp.int32, (384, 256), 1)
    row = to % 24 % 12
    hit = at == to // 24 * 16 + row // 6 * 8 + row % 6
    g = dot(rows[...], gate[...]).astype(bf16)
    u = dot(rows[...], up[...]).astype(bf16)
    is_gate = to % 24 < 12
    both = dot((hit & is_gate).astype(f32).astype(bf16), g)
    both += dot((hit & ~is_gate).astype(f32).astype(bf16), u)
    out[...] = both.astype(bf16)


def hidden_kernel(sums, out):
    total = sums[0].astype(f32)
    for i in range(1, 16):
        total += sums[i].astype(f32)
    g, u = total[:12], total[12:]
    hidden = (g / (1 + jnp.exp(-g)) * u).astype(bf16)
    for i in range(16):
        out[i] = hidden


def in_kernel(place, tok, w0, w1, w2_lo, w2_hi, w3, keep, send):
    z, x = place[0], place[1]

    def rows(s, t):
        if s == 2:
            return (w2_lo, w2_hi)[t // 2][t % 2 * 224:(t % 2 + 1) * 224]
        return (w0, w1, None, w3)[s][t * 224:(t + 1) * 224]

    for odd in range(2):
        acc = jnp.zeros((512, 256), f32)
        for s in (odd, odd + 2):
            a = ((x + 4 - s) % 4) // 2
            for t in range(4):
                acc += dot(tok[2 * ((z + 4 - t) % 4) + a][:, :224], rows(s, t))
        f = (x + odd) % 2
        cols = pl.ds(pl.multiple_of(f * 256, 256), 256)
        keep[:, cols] = acc[:256]
        send[:, cols] = acc[256:].astype(bf16)


def out_kernel(hid, down, spread, slots, out):
    acc = lax.dot_general(slots[...], spread[...], (((0,), (0,)), ((), ())),
                          preferred_element_type=f32)
    for y in range(8):
        acc += dot_t(down[:, y * 256:(y + 1) * 256], hid[y])
    out[...] = acc.astype(bf16)


def body(tokens, shared_gate, shared_up, shared_down, expert_gate, expert_up,
         expert_down, hit_rows, hit_counts, hit_weights):
    core = lax.axis_index("c")
    expert = lax.axis_index(EXP)
    x, z = lax.axis_index("x"), lax.axis_index("z")
    first = core == 0

    lo, hi = tokens[:, :224], tokens[:, 224:]
    tok_own = jnp.pad(jnp.where(first, lo, hi), ((0, 0), (0, 32)))
    tok_other = swap(jnp.pad(jnp.where(first, hi, lo), ((0, 0), (0, 32))), "c")
    w = jnp.concatenate([shared_gate, shared_up], axis=1)
    pieces = []
    for s in range(4):
        turn = []
        for k in range(4):
            for i in range(4):
                for j in range(2):
                    turn.append((8 * k + 2 * i + j,
                                 8 * ((k + s) % 4) + 2 * ((i & 2) | j) + (i & 1)))
        pieces.append(lax.ppermute(w, ("z", "x", "h"), turn))

    def chip_rows(v):
        lo, hi = v[:, :1024], v[:, 1024:]
        own = jnp.where(first, lo, hi)
        got = swap(jnp.where(first, hi, lo), "c")
        return jnp.concatenate(
            [jnp.where(first, own, got), jnp.where(first, got, own)], axis=0)

    g_w, u_w = chip_rows(expert_gate[0]), chip_rows(expert_up[0])
    d_w = chip_rows(expert_down[0].T)

    ids = jnp.pad(hit_rows[0], ((0, 0), (0, 2)), constant_values=-1).reshape(128)
    spread = (ids[:, None] == jnp.arange(256, dtype=jnp.int32)[None, :]).astype(bf16)
    picked = call(pick_kernel, [((128, 448), bf16)], spread, tokens.T)[0].reshape(16, 8, 448)
    mine = exchange(picked, EXP)
    tok = call(stack_kernel, [((512, 256), bf16)], tok_own, tok_other)[0]
    tok = lax.all_gather(tok, "y", axis=0, tiled=True).reshape(8, 512, 256)
    w = call(stack_kernel, [((896, 256), bf16)], *pieces)[0]
    both = call(double_kernel, [((16, 2, 8, 448), bf16)], mine)[0]
    left = lax.ppermute(w, "x", [(i, (i + 1) % 4) for i in range(4)])
    right = lax.ppermute(w, "x", [(i, (i + 3) % 4) for i in range(4)])
    arrived = exchange(both.reshape(32, 8, 448), CTX).reshape(256, 448)
    far = [lax.ppermute(left[:448], "x", [(i, (i + 1) % 4) for i in range(4)]),
           lax.ppermute(right[448:], "x", [(i, (i + 3) % 4) for i in range(4)])]

    parts = call(expert_kernel, [((384, 1024), bf16)], arrived, g_w, u_w,
                 after=[left, right])[0].reshape(16, 24, 1024)
    sums = exchange(parts, CHIP)
    place = jnp.stack([z, x]).astype(jnp.int32)
    part, send = call(in_kernel, [((256, 512), f32), ((256, 512), bf16)],
                      place, tok, w, left, *far, right, scalars=1, after=[parts])
    part = part + swap(send, "c").astype(f32)
    part = part + swap(part.astype(bf16), "h").astype(f32)
    sh = jnp.concatenate(
        [jax.nn.silu(part[:, i:i + 128]) * part[:, i + 128:i + 256] for i in (0, 256)], axis=1)
    sh = lax.all_gather(sh.astype(bf16), "y", axis=0, tiled=True).reshape(8, 256, 256)

    hidden = call(hidden_kernel, [((16, 12, 1024), bf16)], sums)[0]
    hidden = exchange(hidden, CHIP).reshape(192, 1024)
    back = dot_t(hidden, d_w).astype(bf16).reshape(32, 6, 448)
    back = exchange(jnp.pad(back, ((0, 0), (0, 2), (0, 0))), CTX)
    back = jnp.sum(back.astype(f32).reshape(16, 2, 8, 448), axis=1)
    live = jnp.arange(6, dtype=jnp.int32)[None, :] < hit_counts[0][:, None]
    weights = jnp.pad(jnp.where(live, hit_weights[0], 0.0), ((0, 0), (0, 2)))
    weight = lax.dynamic_index_in_dim(weights, expert, 0, keepdims=False)
    back = (back * weight[None, :, None]).astype(bf16)
    slots = exchange(back, EXP).reshape(128, 448)

    out = pl.pallas_call(
        out_kernel, out_shape=jax.ShapeDtypeStruct((448, 256), bf16),
        compiler_params=VMEM,
    )(sh, shared_down.T, spread, slots)
    return out.T


def solution(mesh):
    fine = Mesh(mesh.devices.reshape(4, 4, 2, 8, 2), ("z", "x", "c", "y", "h"))
    placed = (
        P(CTX, EXP),
        P(CTX, EXP),
        P(CTX, EXP),
        P(None, EXP),
        P(EXP, CTX, None),
        P(EXP, CTX, None),
        P(EXP, None, CTX),
        P(CTX, None, None),
        P(CTX, None),
        P(CTX, None, None),
    )
    return jax.shard_map(
        body, mesh=fine, in_specs=placed, out_specs=P(CTX, EXP), check_vma=False)
```

time: 292 us -> 202 us (0.69)
  the two profiles are of different devices: /device:TPU:32 before, /device:TPU:1 now
where the time goes in v2:
time: 202 us; the launch traced here: 201 us
  starting transfers between devices  91.4 us (45%)
  waiting for transfers between devices  52.7 us (26%)
  blocking collectives  20.3 us (10%)
  between operations  14 us (7%)
  Pallas kernels  8.8 us (4%)
  other arithmetic  7.8 us (4%)
  local copies, waits for them, and re-layouts  5.53 us (3%)
    all_to_all x5, starting transfers between devices, exchange(): return lax.all_to_all(v, axes, 0, 0, tiled=True)  39.2 us
    all_to_all x5, waiting for transfers between devices, exchange(): return lax.all_to_all(v, axes, 0, 0, tiled=True)  34.9 us
    ppermute x6, starting transfers between devices, swap(): return lax.ppermute(v, axis, [(0, 1), (1, 0)])  22 us
    all_to_all x1, blocking collectives, exchange(): return lax.all_to_all(v, axes, 0, 0, tiled=True)  20.3 us
    ppermute x4, starting transfers between devices, body(): pieces.append(lax.ppermute(w, ('z', 'x', 'h'), turn))  10.9 us
    ppermute x1, starting transfers between devices, body(): left = lax.ppermute(w, 'x', [(i, (i + 1) % 4) for i in range(4)])  9.3 us
    ppermute x1, waiting for transfers between devices, body(): lax.ppermute(left[:448], 'x', [(i, (i + 1) % 4) for i in range(4)])  8.17 us
    pallas_call x7, Pallas kernels, call(): pl.pallas_call(run, out_shape=[jax.ShapeDtypeStruct(*v) for v in shapes],...  7.38 us
  transfers between devices with their start and end apart: 21, of which 9 were waited for; matrix products, arithmetic and copies ran while one was open for 5% of the time, Pallas kernels for 3%

profile of v2, /device:TPU:1, one launch (start us, length us, event | category | flops | bytes accessed | tf_op | source)
XLA Modules:
  0.0 201.0 jit_solution(8476259797442153569)
XLA Ops:
  6.5 1.0 fusion.8
  7.9 8.9 %collective-permute-start = (bf16[256,256]{1,0:T(8,128)(2,1)S(1)}, bf16[256,256]{1,0:T(8,128)(2,1)S(1)}, u32[]{:S(2)}, u32[]{:S(2)}) collective-permute-start(bf16[256,256]{1,0:T(8,128)(2,1)S(1)} %pad.20), channel_id=1, source_target_pairs={{0,16},{16,0},{1,17},{17,1},{2,18},{18,2},{3,19},{19,3},{4,20},{20... | collective-permute-start | bytes 393224 | tf_op jit(solution)/shard_map/ppermute | solution.py:24
  16.9 0.9 collective-permute-done.refs_1_
  17.8 0.7 shard_map.100
  18.6 0.8 broadcast_select_fusion.6
  19.4 2.3 %collective-permute-start.10 = (bf16[224,1024]{1,0:T(8,128)(2,1)}, bf16[224,1024]{1,0:T(8,128)(2,1)}, u32[]{:S(2)}, u32[]{:S(2)}) collective-permute-start(bf16[224,1024]{1,0:T(8,128)(2,1)} %broadcast_select_fusion.6), channel_id=1, source_target_pairs={{0,16},{16,0},{1,17},{17,1},{2,18},{18,2},{3,19},{19,3},{4,20},{20... | collective-permute-start | bytes 1376264 | tf_op jit(solution)/shard_map/ppermute | solution.py:24
  21.7 0.7 collective-permute-start.1
  22.7 0.9 shard_map.102
  23.6 11.2 %all-to-all-start = ((bf16[16,8,448]{2,1,0:T(8,128)(2,1)}), bf16[16,8,448]{2,1,0:T(8,128)(2,1)S(1)}, u32[]{:S(2)}, u32[]{:S(2)}) async-start(bf16[16,8,448]{2,1,0:T(8,128)(2,1)} %bitcast.4), calls=%async_computation | async-start | bytes 262144 | tf_op jit(solution)/shard_map/all_to_all | solution.py:16
  34.9 0.8 broadcast_select_fusion.10
  35.7 2.3 %collective-permute-start.9 = (bf16[224,1024]{1,0:T(8,128)(2,1)}, bf16[224,1024]{1,0:T(8,128)(2,1)}, u32[]{:S(2)}, u32[]{:S(2)}) collective-permute-start(bf16[224,1024]{1,0:T(8,128)(2,1)} %broadcast_select_fusion.10), channel_id=1, source_target_pairs={{0,16},{16,0},{1,17},{17,1},{2,18},{18,2},{3,19},{19,3},{4,20},{20... | collective-permute-start | bytes 1376264 | tf_op jit(solution)/shard_map/ppermute | solution.py:24
  38.0 3.1 %collective-permute-start.2 = (bf16[224,256]{1,0:T(8,128)(2,1)S(1)}, bf16[224,256]{1,0:T(8,128)(2,1)S(1)}, u32[]{:S(2)}, u32[]{:S(2)}) collective-permute-start(bf16[224,256]{1,0:T(8,128)(2,1)S(1)} %constant_dynamic-update-slice_fusion), channel_id=1, source_target_pairs={{0,128},{1,160},{32,129},{33,161},{64,192},{65,224},{96,193},{97,2... | collective-permute-start | bytes 344072 | tf_op jit(solution)/shard_map/ppermute | solution.py:135
  41.1 4.5 %collective-permute-start.3 = (bf16[224,256]{1,0:T(8,128)(2,1)S(1)}, bf16[224,256]{1,0:T(8,128)(2,1)S(1)}, u32[]{:S(2)}, u32[]{:S(2)}) collective-permute-start(bf16[224,256]{1,0:T(8,128)(2,1)S(1)} %constant_dynamic-update-slice_fusion), channel_id=1, source_target_pairs={{0,256},{1,288},{32,257},{33,289},{64,320},{65,352},{96,321},{97,3... | collective-permute-start | bytes 344072 | tf_op jit(solution)/shard_map/ppermute | solution.py:135
  45.7 2.5 %collective-permute-start.4 = (bf16[224,256]{1,0:T(8,128)(2,1)S(1)}, bf16[224,256]{1,0:T(8,128)(2,1)S(1)}, u32[]{:S(2)}, u32[]{:S(2)}) collective-permute-start(bf16[224,256]{1,0:T(8,128)(2,1)S(1)} %constant_dynamic-update-slice_fusion), channel_id=1, source_target_pairs={{0,384},{1,416},{32,385},{33,417},{64,448},{65,480},{96,449},{97,4... | collective-permute-start | bytes 344072 | tf_op jit(solution)/shard_map/ppermute | solution.py:135
  48.3 0.9 collective-permute-done.2.refs_1_
  49.2 5.2 %collective-permute-done.3.refs_2_ = bf16[224,256]{1,0:T(8,128)(2,1)S(1)} collective-permute-done((bf16[224,256]{1,0:T(8,128)(2,1)S(1)}, bf16[224,256]{1,0:T(8,128)(2,1)S(1)}, u32[]{:S(2)}, u32[]{:S(2)}) %collective-permute-start.3) | collective-permute-done | bytes 114720 | tf_op jit(solution)/shard_map/ppermute | solution.py:135
  54.4 9.3 %collective-permute-start.5 = (bf16[896,256]{1,0:T(8,128)(2,1)S(1)}, bf16[896,256]{1,0:T(8,128)(2,1)S(1)}, u32[]{:S(2)}, u32[]{:S(2)}) collective-permute-start(bf16[896,256]{1,0:T(8,128)(2,1)S(1)} %shard_map.101.refs_2_), channel_id=1, source_target_pairs={{0,32},{32,64},{64,96},{96,0},{1,33},{33,65},{65,97},{97,1},{2,34}... | collective-permute-start | bytes 1376264 | tf_op jit(solution)/shard_map/ppermute | solution.py:155
  63.7 3.5 %collective-permute-start.7 = (bf16[896,256]{1,0:T(8,128)(2,1)S(1)}, bf16[896,256]{1,0:T(8,128)(2,1)S(1)}, u32[]{:S(2)}, u32[]{:S(2)}) collective-permute-start(bf16[896,256]{1,0:T(8,128)(2,1)S(1)} %shard_map.101.refs_2_), channel_id=1, source_target_pairs={{0,96},{32,0},{64,32},{96,64},{1,97},{33,1},{65,33},{97,65},{2,98}... | collective-permute-start | bytes 1376264 | tf_op jit(solution)/shard_map/ppermute | solution.py:156
  67.3 0.7 shard_map.103
  68.0 10.7 %all-to-all-start.1 = ((bf16[32,8,448]{2,1,0:T(8,128)(2,1)}), bf16[32,8,448]{2,1,0:T(8,128)(2,1)S(1)}, u32[]{:S(2)}, u32[]{:S(2)}) async-start(bf16[32,8,448]{2,1,0:T(8,128)(2,1)} %bitcast.5), calls=%async_computation.1 | async-start | bytes 524288 | tf_op jit(solution)/shard_map/all_to_all | solution.py:16
  78.7 1.1 broadcast_select_fusion.5
  79.8 1.1 broadcast_select_fusion.9
  81.1 8.7 %all-to-all-done.1 = bf16[32,8,448]{2,1,0:T(8,128)(2,1)S(1)} async-done(((bf16[32,8,448]{2,1,0:T(8,128)(2,1)}), bf16[32,8,448]{2,1,0:T(8,128)(2,1)S(1)}, u32[]{:S(2)}, u32[]{:S(2)}) %all-to-all-start.1) | async-done | bytes 229408 | tf_op jit(solution)/shard_map/all_to_all | solution.py:16
  89.8 2.3 %shard_map.104 = bf16[384,1024]{1,0:T(8,128)(2,1)} custom-call(bf16[256,448]{1,0:T(8,128)(2,1)S(1)} %bitcast.29, bf16[448,1024]{1,0:T(8,128)(2,1)S(1)} %get-tuple-element.21.refs_1_, bf16[448,1024]{1,0:T(8,128)(2,1)S(1)} %get-tuple-element.22.refs_2_, bf16[896,256]{1,0:T(8,128)(2,1)S(1)} %collective-permute-done.5.refs_3_, ...), custom_call_target="tpu_custom_call" | custom-call | tf_op jit(solution)/shard_map/pallas_call | solution.py:44
  92.1 3.6 %all-to-all-start.2 = ((bf16[16,24,1024]{2,1,0:T(8,128)(2,1)}), bf16[16,24,1024]{2,1,0:T(8,128)(2,1)S(1)}, u32[]{:S(2)}, u32[]{:S(2)}) async-start(bf16[16,24,1024]{2,1,0:T(8,128)(2,1)} %bitcast.9.refs_7_), calls=%async_computation.2 | async-start | bytes 1572864 | tf_op jit(solution)/shard_map/all_to_all | solution.py:16
  95.7 3.1 %collective-permute-start.6 = (bf16[448,256]{1,0:T(8,128)(2,1)S(1)}, bf16[448,256]{1,0:T(8,128)(2,1)S(1)}, u32[]{:S(2)}, u32[]{:S(2)}) collective-permute-start(bf16[448,256]{1,0:T(8,128)(2,1)S(1)} %slice.56), channel_id=1, source_target_pairs={{0,32},{32,64},{64,96},{96,0},{1,33},{33,65},{65,97},{97,1},{2,34}... | collective-permute-start | bytes 688136 | tf_op jit(solution)/shard_map/ppermute | solution.py:158
  98.9 3.3 %collective-permute-start.8 = (bf16[448,256]{1,0:T(8,128)(2,1)S(1)}, bf16[448,256]{1,0:T(8,128)(2,1)S(1)}, u32[]{:S(2)}, u32[]{:S(2)}) collective-permute-start(bf16[448,256]{1,0:T(8,128)(2,1)S(1)} %slice.57), channel_id=1, source_target_pairs={{0,96},{32,0},{64,32},{96,64},{1,97},{33,1},{65,33},{97,65},{2,98}... | collective-permute-start | bytes 688136 | tf_op jit(solution)/shard_map/ppermute | solution.py:159
  102.3 8.2 %collective-permute-done.6.refs_4_ = bf16[448,256]{1,0:T(8,128)(2,1)S(1)} collective-permute-done((bf16[448,256]{1,0:T(8,128)(2,1)S(1)}, bf16[448,256]{1,0:T(8,128)(2,1)S(1)}, u32[]{:S(2)}, u32[]{:S(2)}) %collective-permute-start.6) | collective-permute-done | bytes 229408 | tf_op jit(solution)/shard_map/ppermute | solution.py:158
  110.5 1.4 collective-permute-done.8.refs_5_
  111.9 1.6 copy-done
  113.5 1.8 shard_map.105
  115.3 2.6 %collective-permute-start.11 = (bf16[256,512]{1,0:T(8,128)(2,1)S(1)}, bf16[256,512]{1,0:T(8,128)(2,1)S(1)}, u32[]{:S(2)}, u32[]{:S(2)}) collective-permute-start(bf16[256,512]{1,0:T(8,128)(2,1)S(1)} %get-tuple-element.8), channel_id=1, source_target_pairs={{0,16},{16,0},{1,17},{17,1},{2,18},{18,2},{3,19},{19,3},{4,20},{20... | collective-permute-start | bytes 786440 | tf_op jit(solution)/shard_map/ppermute | solution.py:24
  117.8 1.1 collective-permute-done.11
  119.0 0.8 fusion.3
  119.7 3.4 %collective-permute-start.12 = (bf16[256,512]{1,0:T(8,128)(2,1)}, bf16[256,512]{1,0:T(8,128)(2,1)}, u32[]{:S(2)}, u32[]{:S(2)}) collective-permute-start(bf16[256,512]{1,0:T(8,128)(2,1)} %fusion.3), channel_id=1, source_target_pairs={{0,1},{1,0},{2,3},{3,2},{4,5},{5,4},{6,7},{7,6},{8,9},{9,8},{10,11... | collective-permute-start | bytes 786440 | tf_op jit(solution)/shard_map/ppermute | solution.py:24
  123.1 0.8 broadcast_select_fusion.2
  124.0 2.5 %collective-permute-start.13 = (bf16[224,1024]{1,0:T(8,128)(2,1)}, bf16[224,1024]{1,0:T(8,128)(2,1)S(1)}, u32[]{:S(2)}, u32[]{:S(2)}) collective-permute-start(bf16[224,1024]{1,0:T(8,128)(2,1)} %broadcast_select_fusion.2), channel_id=1, source_target_pairs={{0,16},{16,0},{1,17},{17,1},{2,18},{18,2},{3,19},{19,3},{4,20},{20... | collective-permute-start | bytes 1376264 | tf_op jit(solution)/shard_map/ppermute | solution.py:24
  126.5 1.0 shard_map.106
  127.5 6.9 %all-to-all-start.3 = ((bf16[16,12,1024]{2,1,0:T(8,128)(2,1)}), bf16[16,12,1024]{2,1,0:T(8,128)(2,1)S(1)}, u32[]{:S(2)}, u32[]{:S(2)}) async-start(bf16[16,12,1024]{2,1,0:T(8,128)(2,1)} %shard_map.106), calls=%async_computation.3 | async-start | bytes 1048576 | tf_op jit(solution)/shard_map/all_to_all | solution.py:16
  134.4 1.0 convert_add_fusion
  135.6 0.7 pad_maximum_fusion.2
  136.4 15.3 %all-to-all-done.3 = bf16[16,12,1024]{2,1,0:T(8,128)(2,1)S(1)} async-done(((bf16[16,12,1024]{2,1,0:T(8,128)(2,1)}), bf16[16,12,1024]{2,1,0:T(8,128)(2,1)S(1)}, u32[]{:S(2)}, u32[]{:S(2)}) %all-to-all-start.3) | async-done | bytes 393248 | tf_op jit(solution)/shard_map/all_to_all | solution.py:16
  152.4 0.8 pad.22
  153.1 6.8 %all-to-all-start.4 = ((bf16[32,8,448]{2,1,0:T(8,128)(2,1)}), bf16[32,8,448]{2,1,0:T(8,128)(2,1)S(1)}, u32[]{:S(2)}, u32[]{:S(2)}) async-start(bf16[32,8,448]{2,1,0:T(8,128)(2,1)} %pad.22), calls=%async_computation.4 | async-start | bytes 524288 | tf_op jit(solution)/shard_map/all_to_all | solution.py:16
  160.1 10.9 %all-to-all-done.4 = bf16[32,8,448]{2,1,0:T(8,128)(2,1)S(1)} async-done(((bf16[32,8,448]{2,1,0:T(8,128)(2,1)}), bf16[32,8,448]{2,1,0:T(8,128)(2,1)S(1)}, u32[]{:S(2)}, u32[]{:S(2)}) %all-to-all-start.4) | async-done | bytes 229408 | tf_op jit(solution)/shard_map/all_to_all | solution.py:16
  171.2 20.3 %all_to_all.30 = bf16[16,8,448]{2,1,0:T(8,128)(2,1)S(1)} all-to-all(bf16[16,8,448]{2,1,0:T(8,128)(2,1)S(1)} %multiply_convert_fusion), channel_id=1, replica_groups=mesh['z'=4,'x'=4,'c'=2,'y'=8,'h'=2] {'y','h'}, dimensions={0} | all-to-all | bytes 229376 | tf_op jit(solution)/shard_map/all_to_all | solution.py:16
  191.5 1.2 copy-done.2
  192.7 1.4 shard_map.107
  (65 shorter events, 2.1 us)
Async XLA Ops:
  6.5 12.0 %copy-start.4 = (bf16[1,224,2048]{2,1,0:T(8,128)(2,1)S(1)}, bf16[1,224,2048]{2,1,0:T(8,128)(2,1)}, u32[]{:S(2)}) copy-start(bf16[1,224,2048]{2,1,0:T(8,128)(2,1)} %param.15) | copy-start | bytes 2752516
  6.5 105.3 %all-gather.3.cloned.1.call-start = ((), (), s32[]{:S(2)}) async-start(), calls=%async_computation.6 | async-start | bytes 2359296 | tf_op jit(solution)/shard_map/all_gather | solution.py:152
  7.6 14.1 %copy-start.8 = (bf16[224,128]{1,0:T(8,128)(2,1)S(1)}, bf16[224,128]{1,0:T(8,128)(2,1)}, u32[]{:S(2)}) copy-start(bf16[224,128]{1,0:T(8,128)(2,1)} %param.11) | copy-start | bytes 172036
  7.7 14.0 %copy-start.9 = (bf16[224,128]{1,0:T(8,128)(2,1)S(1)}, bf16[224,128]{1,0:T(8,128)(2,1)}, u32[]{:S(2)}) copy-start(bf16[224,128]{1,0:T(8,128)(2,1)} %param.12) | copy-start | bytes 172036
  7.7 14.7 %copy-start.10 = (s32[1,16,6]{1,0,2:T(1,128)S(1)}, s32[1,16,6]{1,0,2:T(1,128)}, u32[]{:S(2)}) copy-start(s32[1,16,6]{1,0,2:T(1,128)} %param.17) | copy-start | bytes 1156
  7.8 14.9 %copy-start.3 = (bf16[256,448]{0,1:T(8,128)(2,1)S(1)}, bf16[256,448]{0,1:T(8,128)(2,1)}, u32[]{:S(2)}) copy-start(bf16[256,448]{0,1:T(8,128)(2,1)} %param.10) | copy-start | bytes 688132
  7.9 27.0 %copy-start.5 = (bf16[1,224,2048]{2,1,0:T(8,128)(2,1)S(1)}, bf16[1,224,2048]{2,1,0:T(8,128)(2,1)}, u32[]{:S(2)}) copy-start(bf16[1,224,2048]{2,1,0:T(8,128)(2,1)} %param.14) | copy-start | bytes 2752516
  7.9 9.9 %collective-permute-start = (bf16[256,256]{1,0:T(8,128)(2,1)S(1)}, bf16[256,256]{1,0:T(8,128)(2,1)S(1)}, u32[]{:S(2)}, u32[]{:S(2)}) collective-permute-start(bf16[256,256]{1,0:T(8,128)(2,1)S(1)} %pad.20), channel_id=1, source_target_pairs={{0,16},{16,0},{1,17},{17,1},{2,18},{18,2},{3,19},{19,3},{4,20},{20... | collective-permute-start | bytes 393224 | tf_op jit(solution)/shard_map/ppermute | solution.py:24
  19.4 59.3 %collective-permute-start.10 = (bf16[224,1024]{1,0:T(8,128)(2,1)}, bf16[224,1024]{1,0:T(8,128)(2,1)}, u32[]{:S(2)}, u32[]{:S(2)}) collective-permute-start(bf16[224,1024]{1,0:T(8,128)(2,1)} %broadcast_select_fusion.6), channel_id=1, source_target_pairs={{0,16},{16,0},{1,17},{17,1},{2,18},{18,2},{3,19},{19,3},{4,20},{20... | collective-permute-start | bytes 1376264 | tf_op jit(solution)/shard_map/ppermute | solution.py:24
  21.7 24.0 %collective-permute-start.1 = (bf16[224,256]{1,0:T(8,128)(2,1)S(1)}, bf16[224,256]{1,0:T(8,128)(2,1)S(1)}, u32[]{:S(2)}, u32[]{:S(2)}) collective-permute-start(bf16[224,256]{1,0:T(8,128)(2,1)S(1)} %constant_dynamic-update-slice_fusion), channel_id=1, source_target_pairs={{0,0},{1,32},{32,1},{33,33},{64,64},{65,96},{96,65},{97,97},{128,1... | collective-permute-start | bytes 344072 | tf_op jit(solution)/shard_map/ppermute | solution.py:135
  23.6 43.7 %all-to-all-start = ((bf16[16,8,448]{2,1,0:T(8,128)(2,1)}), bf16[16,8,448]{2,1,0:T(8,128)(2,1)S(1)}, u32[]{:S(2)}, u32[]{:S(2)}) async-start(bf16[16,8,448]{2,1,0:T(8,128)(2,1)} %bitcast.4), calls=%async_computation | async-start | bytes 262144 | tf_op jit(solution)/shard_map/all_to_all | solution.py:16
  35.7 44.1 %collective-permute-start.9 = (bf16[224,1024]{1,0:T(8,128)(2,1)}, bf16[224,1024]{1,0:T(8,128)(2,1)}, u32[]{:S(2)}, u32[]{:S(2)}) collective-permute-start(bf16[224,1024]{1,0:T(8,128)(2,1)} %broadcast_select_fusion.10), channel_id=1, source_target_pairs={{0,16},{16,0},{1,17},{17,1},{2,18},{18,2},{3,19},{19,3},{4,20},{20... | collective-permute-start | bytes 1376264 | tf_op jit(solution)/shard_map/ppermute | solution.py:24
  38.0 11.1 %collective-permute-start.2 = (bf16[224,256]{1,0:T(8,128)(2,1)S(1)}, bf16[224,256]{1,0:T(8,128)(2,1)S(1)}, u32[]{:S(2)}, u32[]{:S(2)}) collective-permute-start(bf16[224,256]{1,0:T(8,128)(2,1)S(1)} %constant_dynamic-update-slice_fusion), channel_id=1, source_target_pairs={{0,128},{1,160},{32,129},{33,161},{64,192},{65,224},{96,193},{97,2... | collective-permute-start | bytes 344072 | tf_op jit(solution)/shard_map/ppermute | solution.py:135
  41.1 13.3 %collective-permute-start.3 = (bf16[224,256]{1,0:T(8,128)(2,1)S(1)}, bf16[224,256]{1,0:T(8,128)(2,1)S(1)}, u32[]{:S(2)}, u32[]{:S(2)}) collective-permute-start(bf16[224,256]{1,0:T(8,128)(2,1)S(1)} %constant_dynamic-update-slice_fusion), channel_id=1, source_target_pairs={{0,256},{1,288},{32,257},{33,289},{64,320},{65,352},{96,321},{97,3... | collective-permute-start | bytes 344072 | tf_op jit(solution)/shard_map/ppermute | solution.py:135
  45.7 8.7 %collective-permute-start.4 = (bf16[224,256]{1,0:T(8,128)(2,1)S(1)}, bf16[224,256]{1,0:T(8,128)(2,1)S(1)}, u32[]{:S(2)}, u32[]{:S(2)}) collective-permute-start(bf16[224,256]{1,0:T(8,128)(2,1)S(1)} %constant_dynamic-update-slice_fusion), channel_id=1, source_target_pairs={{0,384},{1,416},{32,385},{33,417},{64,448},{65,480},{96,449},{97,4... | collective-permute-start | bytes 344072 | tf_op jit(solution)/shard_map/ppermute | solution.py:135
  54.4 26.6 %collective-permute-start.5 = (bf16[896,256]{1,0:T(8,128)(2,1)S(1)}, bf16[896,256]{1,0:T(8,128)(2,1)S(1)}, u32[]{:S(2)}, u32[]{:S(2)}) collective-permute-start(bf16[896,256]{1,0:T(8,128)(2,1)S(1)} %shard_map.101.refs_2_), channel_id=1, source_target_pairs={{0,32},{32,64},{64,96},{96,0},{1,33},{33,65},{65,97},{97,1},{2,34}... | collective-permute-start | bytes 1376264 | tf_op jit(solution)/shard_map/ppermute | solution.py:155
  63.7 17.3 %collective-permute-start.7 = (bf16[896,256]{1,0:T(8,128)(2,1)S(1)}, bf16[896,256]{1,0:T(8,128)(2,1)S(1)}, u32[]{:S(2)}, u32[]{:S(2)}) collective-permute-start(bf16[896,256]{1,0:T(8,128)(2,1)S(1)} %shard_map.101.refs_2_), channel_id=1, source_target_pairs={{0,96},{32,0},{64,32},{96,64},{1,97},{33,1},{65,33},{97,65},{2,98}... | collective-permute-start | bytes 1376264 | tf_op jit(solution)/shard_map/ppermute | solution.py:156
  68.0 21.8 %all-to-all-start.1 = ((bf16[32,8,448]{2,1,0:T(8,128)(2,1)}), bf16[32,8,448]{2,1,0:T(8,128)(2,1)S(1)}, u32[]{:S(2)}, u32[]{:S(2)}) async-start(bf16[32,8,448]{2,1,0:T(8,128)(2,1)} %bitcast.5), calls=%async_computation.1 | async-start | bytes 524288 | tf_op jit(solution)/shard_map/all_to_all | solution.py:16
  92.1 34.4 %all-to-all-start.2 = ((bf16[16,24,1024]{2,1,0:T(8,128)(2,1)}), bf16[16,24,1024]{2,1,0:T(8,128)(2,1)S(1)}, u32[]{:S(2)}, u32[]{:S(2)}) async-start(bf16[16,24,1024]{2,1,0:T(8,128)(2,1)} %bitcast.9.refs_7_), calls=%async_computation.2 | async-start | bytes 1572864 | tf_op jit(solution)/shard_map/all_to_all | solution.py:16
  95.7 14.8 %collective-permute-start.6 = (bf16[448,256]{1,0:T(8,128)(2,1)S(1)}, bf16[448,256]{1,0:T(8,128)(2,1)S(1)}, u32[]{:S(2)}, u32[]{:S(2)}) collective-permute-start(bf16[448,256]{1,0:T(8,128)(2,1)S(1)} %slice.56), channel_id=1, source_target_pairs={{0,32},{32,64},{64,96},{96,0},{1,33},{33,65},{65,97},{97,1},{2,34}... | collective-permute-start | bytes 688136 | tf_op jit(solution)/shard_map/ppermute | solution.py:158
  98.9 13.0 %collective-permute-start.8 = (bf16[448,256]{1,0:T(8,128)(2,1)S(1)}, bf16[448,256]{1,0:T(8,128)(2,1)S(1)}, u32[]{:S(2)}, u32[]{:S(2)}) collective-permute-start(bf16[448,256]{1,0:T(8,128)(2,1)S(1)} %slice.57), channel_id=1, source_target_pairs={{0,96},{32,0},{64,32},{96,64},{1,97},{33,1},{65,33},{97,65},{2,98}... | collective-permute-start | bytes 688136 | tf_op jit(solution)/shard_map/ppermute | solution.py:159
  111.9 1.6 copy-start
  113.5 9.7 %copy-start.6 = (bf16[1,2048,224]{1,2,0:T(8,128)(2,1)S(1)}, bf16[1,2048,224]{1,2,0:T(8,128)(2,1)}, u32[]{:S(2)}) copy-start(bf16[1,2048,224]{1,2,0:T(8,128)(2,1)} %param.16) | copy-start | bytes 2752516
  115.3 3.7 %collective-permute-start.11 = (bf16[256,512]{1,0:T(8,128)(2,1)S(1)}, bf16[256,512]{1,0:T(8,128)(2,1)S(1)}, u32[]{:S(2)}, u32[]{:S(2)}) collective-permute-start(bf16[256,512]{1,0:T(8,128)(2,1)S(1)} %get-tuple-element.8), channel_id=1, source_target_pairs={{0,16},{16,0},{1,17},{17,1},{2,18},{18,2},{3,19},{19,3},{4,20},{20... | collective-permute-start | bytes 786440 | tf_op jit(solution)/shard_map/ppermute | solution.py:24
  119.7 14.7 %collective-permute-start.12 = (bf16[256,512]{1,0:T(8,128)(2,1)}, bf16[256,512]{1,0:T(8,128)(2,1)}, u32[]{:S(2)}, u32[]{:S(2)}) collective-permute-start(bf16[256,512]{1,0:T(8,128)(2,1)} %fusion.3), channel_id=1, source_target_pairs={{0,1},{1,0},{2,3},{3,2},{4,5},{5,4},{6,7},{7,6},{8,9},{9,8},{10,11... | collective-permute-start | bytes 786440 | tf_op jit(solution)/shard_map/ppermute | solution.py:24
  124.0 12.3 %collective-permute-start.13 = (bf16[224,1024]{1,0:T(8,128)(2,1)}, bf16[224,1024]{1,0:T(8,128)(2,1)S(1)}, u32[]{:S(2)}, u32[]{:S(2)}) collective-permute-start(bf16[224,1024]{1,0:T(8,128)(2,1)} %broadcast_select_fusion.2), channel_id=1, source_target_pairs={{0,16},{16,0},{1,17},{17,1},{2,18},{18,2},{3,19},{19,3},{4,20},{20... | collective-permute-start | bytes 1376264 | tf_op jit(solution)/shard_map/ppermute | solution.py:24
  127.5 8.8 %copy-start.7 = (bf16[1,2048,224]{1,2,0:T(8,128)(2,1)S(1)}, bf16[1,2048,224]{1,2,0:T(8,128)(2,1)}, u32[]{:S(2)}) copy-start(bf16[1,2048,224]{1,2,0:T(8,128)(2,1)} %param.16) | copy-start | bytes 2752516
  127.5 24.2 %all-to-all-start.3 = ((bf16[16,12,1024]{2,1,0:T(8,128)(2,1)}), bf16[16,12,1024]{2,1,0:T(8,128)(2,1)S(1)}, u32[]{:S(2)}, u32[]{:S(2)}) async-start(bf16[16,12,1024]{2,1,0:T(8,128)(2,1)} %shard_map.106), calls=%async_computation.3 | async-start | bytes 1048576 | tf_op jit(solution)/shard_map/all_to_all | solution.py:16
  134.4 57.1 %all-gather.5.cloned.1.call-start = ((), (), s32[]{:S(2)}) async-start(), calls=%async_computation.7 | async-start | bytes 1179648 | tf_op jit(solution)/shard_map/all_gather | solution.py:171
  151.8 8.2 %copy-start.11 = (f32[1,16,6]{1,0,2:T(1,128)S(1)}, f32[1,16,6]{1,0,2:T(1,128)}, u32[]{:S(2)}) copy-start(f32[1,16,6]{1,0,2:T(1,128)} %param.19) | copy-start | bytes 1156
  151.8 8.2 %copy-start.12 = (s32[1,16]{1,0:T(1,128)S(1)}, s32[1,16]{1,0:T(1,128)}, u32[]{:S(2)}) copy-start(s32[1,16]{1,0:T(1,128)} %param.18) | copy-start | bytes 196
  152.3 39.2 %copy-start.1 = (bf16[2048,448]{0,1:T(8,128)(2,1)S(1)}, bf16[2048,448]{0,1:T(8,128)(2,1)}, u32[]{:S(2)}) copy-start(bf16[2048,448]{0,1:T(8,128)(2,1)} %param.13) | copy-start | bytes 5505028
  153.1 17.9 %all-to-all-start.4 = ((bf16[32,8,448]{2,1,0:T(8,128)(2,1)}), bf16[32,8,448]{2,1,0:T(8,128)(2,1)S(1)}, u32[]{:S(2)}, u32[]{:S(2)}) async-start(bf16[32,8,448]{2,1,0:T(8,128)(2,1)} %pad.22), calls=%async_computation.4 | async-start | bytes 524288 | tf_op jit(solution)/shard_map/all_to_all | solution.py:16
  191.5 1.2 copy-start.2
Sparse Core Ops, SparseCore 0:
  18.7 40.9 all-gather.2
  137.3 38.3 all-gather.4

commit v3 on v2

--- a/solution.py
+++ b/solution.py
@@ -124,15 +124,12 @@
     tok_own = jnp.pad(jnp.where(first, lo, hi), ((0, 0), (0, 32)))
     tok_other = swap(jnp.pad(jnp.where(first, hi, lo), ((0, 0), (0, 32))), "c")
     w = jnp.concatenate([shared_gate, shared_up], axis=1)
-    pieces = []
-    for s in range(4):
-        turn = []
-        for k in range(4):
-            for i in range(4):
-                for j in range(2):
-                    turn.append((8 * k + 2 * i + j,
-                                 8 * ((k + s) % 4) + 2 * ((i & 2) | j) + (i & 1)))
-        pieces.append(lax.ppermute(w, ("z", "x", "h"), turn))
+    turn = []
+    for i in range(4):
+        for j in range(2):
+            turn.append((2 * i + j, 2 * ((i & 2) | j) + (i & 1)))
+    w = lax.ppermute(w, ("x", "h"), turn)
+    pieces = [w] + [lax.ppermute(w, "z", [(i, (i + s) % 4) for i in range(4)]) for s in range(1, 4)]
 
     def chip_rows(v):
         lo, hi = v[:, :1024], v[:, 1024:]

time: 202 us -> 190 us (0.941)
  waiting for transfers between devices: 52.7 us -> 46.4 us
  other arithmetic: 7.8 us -> 5.06 us
  starting transfers between devices: 91.4 us -> 89.1 us
    ppermute x4, waiting for transfers between devices: 6.15 us -> 0.01 us  [the longest x3 0.01 us: body(): lax.ppermute(w, 'z', [(i, (i + s) % 4) for i in range(4)])]
    ppermute x1, waiting for transfers between devices: 0.01 us -> 6.1 us  [body(): left = lax.ppermute(w, 'x', [(i, (i + 1) % 4) for i in range(4)])]
    ppermute x1, starting transfers between devices: 9.3 us -> 3.43 us  [body(): left = lax.ppermute(w, 'x', [(i, (i + 1) % 4) for i in range(4)])]
    all_to_all x5, waiting for transfers between devices: 34.9 us -> 30.2 us  [exchange(): return lax.all_to_all(v, axes, 0, 0, tiled=True)]
    all_to_all x5, starting transfers between devices: 39.2 us -> 41.5 us  [exchange(): return lax.all_to_all(v, axes, 0, 0, tiled=True)]
    select_n x3, other arithmetic: 2.29 us -> 0.25 us  [chip_rows(): jnp.where(first, own, got)]
  transfers between devices with their start and end apart: 21 -> 21, of which waited for: 9 -> 10; matrix products, arithmetic and copies ran while one was open for 5% -> 4% of each run, Pallas kernels for 3% -> 4%
where the time goes in v3:
time: 190 us; the launch traced here: 189 us
  starting transfers between devices  89.1 us (47%)
  waiting for transfers between devices  46.4 us (24%)
  blocking collectives  19.8 us (10%)
  between operations  14 us (7%)
  Pallas kernels  8.77 us (5%)
  local copies, waits for them, and re-layouts  5.52 us (3%)
  other arithmetic  5.06 us (3%)
    all_to_all x5, starting transfers between devices, exchange(): return lax.all_to_all(v, axes, 0, 0, tiled=True)  41.5 us
    all_to_all x5, waiting for transfers between devices, exchange(): return lax.all_to_all(v, axes, 0, 0, tiled=True)  30.2 us
    ppermute x6, starting transfers between devices, swap(): return lax.ppermute(v, axis, [(0, 1), (1, 0)])  23.6 us
    all_to_all x1, blocking collectives, exchange(): return lax.all_to_all(v, axes, 0, 0, tiled=True)  19.8 us
    ppermute x3, starting transfers between devices, body(): lax.ppermute(w, 'z', [(i, (i + s) % 4) for i in range(4)])  10.2 us
    ppermute x1, waiting for transfers between devices, body(): lax.ppermute(left[:448], 'x', [(i, (i + 1) % 4) for i in range(4)])  7.52 us
    pallas_call x7, Pallas kernels, call(): pl.pallas_call(run, out_shape=[jax.ShapeDtypeStruct(*v) for v in shapes],...  7.35 us
    ppermute x1, waiting for transfers between devices, body(): left = lax.ppermute(w, 'x', [(i, (i + 1) % 4) for i in range(4)])  6.1 us
  transfers between devices with their start and end apart: 21, of which 10 were waited for; matrix products, arithmetic and copies ran while one was open for 4% of the time, Pallas kernels for 4%

profile of v3, /device:TPU:1, one launch (start us, length us, event | category | flops | bytes accessed | tf_op | source)
XLA Modules:
  0.0 189.2 jit_solution(10926463129798810573)
XLA Ops:
  6.5 1.0 fusion.8
  7.9 8.9 %collective-permute-start = (bf16[256,256]{1,0:T(8,128)(2,1)S(1)}, bf16[256,256]{1,0:T(8,128)(2,1)S(1)}, u32[]{:S(2)}, u32[]{:S(2)}) collective-permute-start(bf16[256,256]{1,0:T(8,128)(2,1)S(1)} %pad.20), channel_id=1, source_target_pairs={{0,16},{16,0},{1,17},{17,1},{2,18},{18,2},{3,19},{19,3},{4,20},{20... | collective-permute-start | bytes 393224 | tf_op jit(solution)/shard_map/ppermute | solution.py:24
  16.9 0.9 collective-permute-done.refs_1_
  17.8 0.7 shard_map.100
  18.6 0.8 broadcast_select_fusion.6
  19.4 2.3 %collective-permute-start.10 = (bf16[224,1024]{1,0:T(8,128)(2,1)}, bf16[224,1024]{1,0:T(8,128)(2,1)S(1)}, u32[]{:S(2)}, u32[]{:S(2)}) collective-permute-start(bf16[224,1024]{1,0:T(8,128)(2,1)} %broadcast_select_fusion.6), channel_id=1, source_target_pairs={{0,16},{16,0},{1,17},{17,1},{2,18},{18,2},{3,19},{19,3},{4,20},{20... | collective-permute-start | bytes 1376264 | tf_op jit(solution)/shard_map/ppermute | solution.py:24
  21.7 0.7 collective-permute-start.1
  22.7 0.9 shard_map.102
  23.6 11.2 %all-to-all-start = ((bf16[16,8,448]{2,1,0:T(8,128)(2,1)}), bf16[16,8,448]{2,1,0:T(8,128)(2,1)S(1)}, u32[]{:S(2)}, u32[]{:S(2)}) async-start(bf16[16,8,448]{2,1,0:T(8,128)(2,1)} %bitcast.4), calls=%async_computation | async-start | bytes 262144 | tf_op jit(solution)/shard_map/all_to_all | solution.py:16
  34.8 0.8 broadcast_select_fusion.10
  35.7 2.3 %collective-permute-start.9 = (bf16[224,1024]{1,0:T(8,128)(2,1)}, bf16[224,1024]{1,0:T(8,128)(2,1)S(1)}, u32[]{:S(2)}, u32[]{:S(2)}) collective-permute-start(bf16[224,1024]{1,0:T(8,128)(2,1)} %broadcast_select_fusion.10), channel_id=1, source_target_pairs={{0,16},{16,0},{1,17},{17,1},{2,18},{18,2},{3,19},{19,3},{4,20},{20... | collective-permute-start | bytes 1376264 | tf_op jit(solution)/shard_map/ppermute | solution.py:24
  38.0 3.1 %collective-permute-start.2 = (bf16[224,256]{1,0:T(8,128)(2,1)S(1)}, bf16[224,256]{1,0:T(8,128)(2,1)S(1)}, u32[]{:S(2)}, u32[]{:S(2)}) collective-permute-start(bf16[224,256]{1,0:T(8,128)(2,1)S(1)} %collective-permute-done.1.refs_0_), channel_id=1, source_target_pairs={{0,128},{128,256},{256,384},{384,0},{1,129},{129,257},{257,385},{3... | collective-permute-start | bytes 344072 | tf_op jit(solution)/shard_map/ppermute | solution.py:132
  41.1 4.5 %collective-permute-start.3 = (bf16[224,256]{1,0:T(8,128)(2,1)S(1)}, bf16[224,256]{1,0:T(8,128)(2,1)S(1)}, u32[]{:S(2)}, u32[]{:S(2)}) collective-permute-start(bf16[224,256]{1,0:T(8,128)(2,1)S(1)} %collective-permute-done.1.refs_0_), channel_id=1, source_target_pairs={{0,256},{128,384},{256,0},{384,128},{1,257},{129,385},{257,1},{385... | collective-permute-start | bytes 344072 | tf_op jit(solution)/shard_map/ppermute | solution.py:132
  45.7 2.5 %collective-permute-start.4 = (bf16[224,256]{1,0:T(8,128)(2,1)S(1)}, bf16[224,256]{1,0:T(8,128)(2,1)S(1)}, u32[]{:S(2)}, u32[]{:S(2)}) collective-permute-start(bf16[224,256]{1,0:T(8,128)(2,1)S(1)} %collective-permute-done.1.refs_0_), channel_id=1, source_target_pairs={{0,384},{128,0},{256,128},{384,256},{1,385},{129,1},{257,129},{385... | collective-permute-start | bytes 344072 | tf_op jit(solution)/shard_map/ppermute | solution.py:132
  48.2 1.3 all-to-all-done.refs_0_
  49.5 0.7 shard_map.103
  50.2 8.9 %all-to-all-start.1 = ((bf16[32,8,448]{2,1,0:T(8,128)(2,1)}), bf16[32,8,448]{2,1,0:T(8,128)(2,1)S(1)}, u32[]{:S(2)}, u32[]{:S(2)}) async-start(bf16[32,8,448]{2,1,0:T(8,128)(2,1)} %bitcast.5), calls=%async_computation.1 | async-start | bytes 524288 | tf_op jit(solution)/shard_map/all_to_all | solution.py:16
  59.2 3.4 %collective-permute-start.5 = (bf16[896,256]{1,0:T(8,128)(2,1)S(1)}, bf16[896,256]{1,0:T(8,128)(2,1)S(1)}, u32[]{:S(2)}, u32[]{:S(2)}) collective-permute-start(bf16[896,256]{1,0:T(8,128)(2,1)S(1)} %shard_map.101.refs_2_), channel_id=1, source_target_pairs={{0,32},{32,64},{64,96},{96,0},{1,33},{33,65},{65,97},{97,1},{2,34}... | collective-permute-start | bytes 1376264 | tf_op jit(solution)/shard_map/ppermute | solution.py:152
  62.7 3.2 %collective-permute-start.7 = (bf16[896,256]{1,0:T(8,128)(2,1)S(1)}, bf16[896,256]{1,0:T(8,128)(2,1)S(1)}, u32[]{:S(2)}, u32[]{:S(2)}) collective-permute-start(bf16[896,256]{1,0:T(8,128)(2,1)S(1)} %shard_map.101.refs_2_), channel_id=1, source_target_pairs={{0,96},{32,0},{64,32},{96,64},{1,97},{33,1},{65,33},{97,65},{2,98}... | collective-permute-start | bytes 1376264 | tf_op jit(solution)/shard_map/ppermute | solution.py:153
  66.2 4.1 %all-to-all-done.1 = bf16[32,8,448]{2,1,0:T(8,128)(2,1)S(1)} async-done(((bf16[32,8,448]{2,1,0:T(8,128)(2,1)}), bf16[32,8,448]{2,1,0:T(8,128)(2,1)S(1)}, u32[]{:S(2)}, u32[]{:S(2)}) %all-to-all-start.1) | async-done | bytes 229408 | tf_op jit(solution)/shard_map/all_to_all | solution.py:16
  70.4 6.1 %collective-permute-done.5.refs_3_ = bf16[896,256]{1,0:T(8,128)(2,1)S(1)} collective-permute-done((bf16[896,256]{1,0:T(8,128)(2,1)S(1)}, bf16[896,256]{1,0:T(8,128)(2,1)S(1)}, u32[]{:S(2)}, u32[]{:S(2)}) %collective-permute-start.5) | collective-permute-done | bytes 458784 | tf_op jit(solution)/shard_map/ppermute | solution.py:152
  76.5 0.2 collective-permute-done.7.refs_4_.refs_6_
  76.6 2.3 %shard_map.104 = bf16[384,1024]{1,0:T(8,128)(2,1)} custom-call(bf16[256,448]{1,0:T(8,128)(2,1)S(1)} %bitcast.29, bf16[448,1024]{1,0:T(8,128)(2,1)S(1)} %get-tuple-element.21.refs_1_, bf16[448,1024]{1,0:T(8,128)(2,1)S(1)} %get-tuple-element.22.refs_2_, bf16[896,256]{1,0:T(8,128)(2,1)S(1)} %collective-permute-done.5.refs_3_, ...), custom_call_target="tpu_custom_call" | custom-call | tf_op jit(solution)/shard_map/pallas_call | solution.py:44
  78.9 6.2 %all-to-all-start.2 = ((bf16[16,24,1024]{2,1,0:T(8,128)(2,1)}), bf16[16,24,1024]{2,1,0:T(8,128)(2,1)S(1)}, u32[]{:S(2)}, u32[]{:S(2)}) async-start(bf16[16,24,1024]{2,1,0:T(8,128)(2,1)} %bitcast.9.refs_7_), calls=%async_computation.2 | async-start | bytes 1572864 | tf_op jit(solution)/shard_map/all_to_all | solution.py:16
  85.1 3.3 %collective-permute-start.6 = (bf16[448,256]{1,0:T(8,128)(2,1)S(1)}, bf16[448,256]{1,0:T(8,128)(2,1)S(1)}, u32[]{:S(2)}, u32[]{:S(2)}) collective-permute-start(bf16[448,256]{1,0:T(8,128)(2,1)S(1)} %slice.56), channel_id=1, source_target_pairs={{0,32},{32,64},{64,96},{96,0},{1,33},{33,65},{65,97},{97,1},{2,34}... | collective-permute-start | bytes 688136 | tf_op jit(solution)/shard_map/ppermute | solution.py:155
  88.4 3.2 %collective-permute-start.8 = (bf16[448,256]{1,0:T(8,128)(2,1)S(1)}, bf16[448,256]{1,0:T(8,128)(2,1)S(1)}, u32[]{:S(2)}, u32[]{:S(2)}) collective-permute-start(bf16[448,256]{1,0:T(8,128)(2,1)S(1)} %slice.57), channel_id=1, source_target_pairs={{0,96},{32,0},{64,32},{96,64},{1,97},{33,1},{65,33},{97,65},{2,98}... | collective-permute-start | bytes 688136 | tf_op jit(solution)/shard_map/ppermute | solution.py:156
  91.7 7.5 %collective-permute-done.6.refs_4_ = bf16[448,256]{1,0:T(8,128)(2,1)S(1)} collective-permute-done((bf16[448,256]{1,0:T(8,128)(2,1)S(1)}, bf16[448,256]{1,0:T(8,128)(2,1)S(1)}, u32[]{:S(2)}, u32[]{:S(2)}) %collective-permute-start.6) | collective-permute-done | bytes 229408 | tf_op jit(solution)/shard_map/ppermute | solution.py:155
  99.2 0.3 collective-permute-done.8.refs_5_
  99.5 1.6 copy-done
  101.1 1.8 shard_map.105
  102.9 4.4 %collective-permute-start.11 = (bf16[256,512]{1,0:T(8,128)(2,1)S(1)}, bf16[256,512]{1,0:T(8,128)(2,1)S(1)}, u32[]{:S(2)}, u32[]{:S(2)}) collective-permute-start(bf16[256,512]{1,0:T(8,128)(2,1)S(1)} %get-tuple-element.8), channel_id=1, source_target_pairs={{0,16},{16,0},{1,17},{17,1},{2,18},{18,2},{3,19},{19,3},{4,20},{20... | collective-permute-start | bytes 786440 | tf_op jit(solution)/shard_map/ppermute | solution.py:24
  107.3 1.1 collective-permute-done.11
  108.5 3.1 %collective-permute-start.12 = (bf16[256,512]{1,0:T(8,128)(2,1)S(1)}, bf16[256,512]{1,0:T(8,128)(2,1)}, u32[]{:S(2)}, u32[]{:S(2)}) collective-permute-start(bf16[256,512]{1,0:T(8,128)(2,1)S(1)} %fusion.3), channel_id=1, source_target_pairs={{0,1},{1,0},{2,3},{3,2},{4,5},{5,4},{6,7},{7,6},{8,9},{9,8},{10,11... | collective-permute-start | bytes 786440 | tf_op jit(solution)/shard_map/ppermute | solution.py:24
  111.6 0.8 broadcast_select_fusion.2
  112.5 2.5 %collective-permute-start.13 = (bf16[224,1024]{1,0:T(8,128)(2,1)}, bf16[224,1024]{1,0:T(8,128)(2,1)S(1)}, u32[]{:S(2)}, u32[]{:S(2)}) collective-permute-start(bf16[224,1024]{1,0:T(8,128)(2,1)} %broadcast_select_fusion.2), channel_id=1, source_target_pairs={{0,16},{16,0},{1,17},{17,1},{2,18},{18,2},{3,19},{19,3},{4,20},{20... | collective-permute-start | bytes 1376264 | tf_op jit(solution)/shard_map/ppermute | solution.py:24
  115.0 1.0 shard_map.106
  116.0 6.7 %all-to-all-start.3 = ((bf16[16,12,1024]{2,1,0:T(8,128)(2,1)}), bf16[16,12,1024]{2,1,0:T(8,128)(2,1)S(1)}, u32[]{:S(2)}, u32[]{:S(2)}) async-start(bf16[16,12,1024]{2,1,0:T(8,128)(2,1)} %shard_map.106), calls=%async_computation.3 | async-start | bytes 1048576 | tf_op jit(solution)/shard_map/all_to_all | solution.py:16
  122.7 1.0 convert_add_fusion
  123.9 0.7 pad_maximum_fusion.2
  124.7 13.9 %all-to-all-done.3 = bf16[16,12,1024]{2,1,0:T(8,128)(2,1)S(1)} async-done(((bf16[16,12,1024]{2,1,0:T(8,128)(2,1)}), bf16[16,12,1024]{2,1,0:T(8,128)(2,1)S(1)}, u32[]{:S(2)}, u32[]{:S(2)}) %all-to-all-start.3) | async-done | bytes 393248 | tf_op jit(solution)/shard_map/all_to_all | solution.py:16
  138.7 0.4 convolution_convert_fusion
  139.3 0.8 pad.22
  140.1 8.5 %all-to-all-start.4 = ((bf16[32,8,448]{2,1,0:T(8,128)(2,1)}), bf16[32,8,448]{2,1,0:T(8,128)(2,1)S(1)}, u32[]{:S(2)}, u32[]{:S(2)}) async-start(bf16[32,8,448]{2,1,0:T(8,128)(2,1)} %pad.22), calls=%async_computation.4 | async-start | bytes 524288 | tf_op jit(solution)/shard_map/all_to_all | solution.py:16
  148.7 0.2 dynamic-slice_reduce_fusion
  148.8 10.9 %all-to-all-done.4 = bf16[32,8,448]{2,1,0:T(8,128)(2,1)S(1)} async-done(((bf16[32,8,448]{2,1,0:T(8,128)(2,1)}), bf16[32,8,448]{2,1,0:T(8,128)(2,1)S(1)}, u32[]{:S(2)}, u32[]{:S(2)}) %all-to-all-start.4) | async-done | bytes 229408 | tf_op jit(solution)/shard_map/all_to_all | solution.py:16
  159.9 19.8 %all_to_all.30 = bf16[16,8,448]{2,1,0:T(8,128)(2,1)S(1)} all-to-all(bf16[16,8,448]{2,1,0:T(8,128)(2,1)S(1)} %multiply_convert_fusion), channel_id=1, replica_groups=mesh['z'=4,'x'=4,'c'=2,'y'=8,'h'=2] {'y','h'}, dimensions={0} | all-to-all | bytes 229376 | tf_op jit(solution)/shard_map/all_to_all | solution.py:16
  179.7 1.2 copy-done.2
  180.9 1.4 shard_map.107
  (66 shorter events, 1.7 us)
Async XLA Ops:
  6.5 12.0 %copy-start.4 = (bf16[1,224,2048]{2,1,0:T(8,128)(2,1)S(1)}, bf16[1,224,2048]{2,1,0:T(8,128)(2,1)}, u32[]{:S(2)}) copy-start(bf16[1,224,2048]{2,1,0:T(8,128)(2,1)} %param.15) | copy-start | bytes 2752516
  6.5 93.0 %all-gather.3.cloned.1.call-start = ((), (), s32[]{:S(2)}) async-start(), calls=%async_computation.6 | async-start | bytes 2359296 | tf_op jit(solution)/shard_map/all_gather | solution.py:149
  7.6 14.1 %copy-start.9 = (bf16[224,128]{1,0:T(8,128)(2,1)S(1)}, bf16[224,128]{1,0:T(8,128)(2,1)}, u32[]{:S(2)}) copy-start(bf16[224,128]{1,0:T(8,128)(2,1)} %param.12) | copy-start | bytes 172036
  7.6 14.1 %copy-start.10 = (bf16[224,128]{1,0:T(8,128)(2,1)S(1)}, bf16[224,128]{1,0:T(8,128)(2,1)}, u32[]{:S(2)}) copy-start(bf16[224,128]{1,0:T(8,128)(2,1)} %param.11) | copy-start | bytes 172036
  7.7 14.7 %copy-start.11 = (s32[1,16,6]{1,0,2:T(1,128)S(1)}, s32[1,16,6]{1,0,2:T(1,128)}, u32[]{:S(2)}) copy-start(s32[1,16,6]{1,0,2:T(1,128)} %param.17) | copy-start | bytes 1156
  7.8 14.8 %copy-start.3 = (bf16[256,448]{0,1:T(8,128)(2,1)S(1)}, bf16[256,448]{0,1:T(8,128)(2,1)}, u32[]{:S(2)}) copy-start(bf16[256,448]{0,1:T(8,128)(2,1)} %param.10) | copy-start | bytes 688132
  7.9 26.9 %copy-start.5 = (bf16[1,224,2048]{2,1,0:T(8,128)(2,1)S(1)}, bf16[1,224,2048]{2,1,0:T(8,128)(2,1)}, u32[]{:S(2)}) copy-start(bf16[1,224,2048]{2,1,0:T(8,128)(2,1)} %param.14) | copy-start | bytes 2752516
  7.9 9.9 %collective-permute-start = (bf16[256,256]{1,0:T(8,128)(2,1)S(1)}, bf16[256,256]{1,0:T(8,128)(2,1)S(1)}, u32[]{:S(2)}, u32[]{:S(2)}) collective-permute-start(bf16[256,256]{1,0:T(8,128)(2,1)S(1)} %pad.20), channel_id=1, source_target_pairs={{0,16},{16,0},{1,17},{17,1},{2,18},{18,2},{3,19},{19,3},{4,20},{20... | collective-permute-start | bytes 393224 | tf_op jit(solution)/shard_map/ppermute | solution.py:24
  19.4 46.5 %collective-permute-start.10 = (bf16[224,1024]{1,0:T(8,128)(2,1)}, bf16[224,1024]{1,0:T(8,128)(2,1)S(1)}, u32[]{:S(2)}, u32[]{:S(2)}) collective-permute-start(bf16[224,1024]{1,0:T(8,128)(2,1)} %broadcast_select_fusion.6), channel_id=1, source_target_pairs={{0,16},{16,0},{1,17},{17,1},{2,18},{18,2},{3,19},{19,3},{4,20},{20... | collective-permute-start | bytes 1376264 | tf_op jit(solution)/shard_map/ppermute | solution.py:24
  21.7 16.3 %collective-permute-start.1 = (bf16[224,256]{1,0:T(8,128)(2,1)S(1)}, bf16[224,256]{1,0:T(8,128)(2,1)S(1)}, u32[]{:S(2)}, u32[]{:S(2)}) collective-permute-start(bf16[224,256]{1,0:T(8,128)(2,1)S(1)} %pad_maximum_fusion.3), channel_id=1, source_target_pairs={{0,0},{1,32},{32,1},{33,33},{64,64},{65,96},{96,65},{97,97},{2,2},... | collective-permute-start | bytes 344072 | tf_op jit(solution)/shard_map/ppermute | solution.py:131
  23.6 26.0 %all-to-all-start = ((bf16[16,8,448]{2,1,0:T(8,128)(2,1)}), bf16[16,8,448]{2,1,0:T(8,128)(2,1)S(1)}, u32[]{:S(2)}, u32[]{:S(2)}) async-start(bf16[16,8,448]{2,1,0:T(8,128)(2,1)} %bitcast.4), calls=%async_computation | async-start | bytes 262144 | tf_op jit(solution)/shard_map/all_to_all | solution.py:16
  35.7 30.3 %collective-permute-start.9 = (bf16[224,1024]{1,0:T(8,128)(2,1)}, bf16[224,1024]{1,0:T(8,128)(2,1)S(1)}, u32[]{:S(2)}, u32[]{:S(2)}) collective-permute-start(bf16[224,1024]{1,0:T(8,128)(2,1)} %broadcast_select_fusion.10), channel_id=1, source_target_pairs={{0,16},{16,0},{1,17},{17,1},{2,18},{18,2},{3,19},{19,3},{4,20},{20... | collective-permute-start | bytes 1376264 | tf_op jit(solution)/shard_map/ppermute | solution.py:24
  38.0 21.1 %collective-permute-start.2 = (bf16[224,256]{1,0:T(8,128)(2,1)S(1)}, bf16[224,256]{1,0:T(8,128)(2,1)S(1)}, u32[]{:S(2)}, u32[]{:S(2)}) collective-permute-start(bf16[224,256]{1,0:T(8,128)(2,1)S(1)} %collective-permute-done.1.refs_0_), channel_id=1, source_target_pairs={{0,128},{128,256},{256,384},{384,0},{1,129},{129,257},{257,385},{3... | collective-permute-start | bytes 344072 | tf_op jit(solution)/shard_map/ppermute | solution.py:132
  41.1 18.0 %collective-permute-start.3 = (bf16[224,256]{1,0:T(8,128)(2,1)S(1)}, bf16[224,256]{1,0:T(8,128)(2,1)S(1)}, u32[]{:S(2)}, u32[]{:S(2)}) collective-permute-start(bf16[224,256]{1,0:T(8,128)(2,1)S(1)} %collective-permute-done.1.refs_0_), channel_id=1, source_target_pairs={{0,256},{128,384},{256,0},{384,128},{1,257},{129,385},{257,1},{385... | collective-permute-start | bytes 344072 | tf_op jit(solution)/shard_map/ppermute | solution.py:132
  45.7 13.5 %collective-permute-start.4 = (bf16[224,256]{1,0:T(8,128)(2,1)S(1)}, bf16[224,256]{1,0:T(8,128)(2,1)S(1)}, u32[]{:S(2)}, u32[]{:S(2)}) collective-permute-start(bf16[224,256]{1,0:T(8,128)(2,1)S(1)} %collective-permute-done.1.refs_0_), channel_id=1, source_target_pairs={{0,384},{128,0},{256,128},{384,256},{1,385},{129,1},{257,129},{385... | collective-permute-start | bytes 344072 | tf_op jit(solution)/shard_map/ppermute | solution.py:132
  50.2 20.1 %all-to-all-start.1 = ((bf16[32,8,448]{2,1,0:T(8,128)(2,1)}), bf16[32,8,448]{2,1,0:T(8,128)(2,1)S(1)}, u32[]{:S(2)}, u32[]{:S(2)}) async-start(bf16[32,8,448]{2,1,0:T(8,128)(2,1)} %bitcast.5), calls=%async_computation.1 | async-start | bytes 524288 | tf_op jit(solution)/shard_map/all_to_all | solution.py:16
  59.1 6.8 %copy-start.6 = (bf16[1,224,2048]{2,1,0:T(8,128)(2,1)S(1)}, bf16[1,224,2048]{2,1,0:T(8,128)(2,1)}, u32[]{:S(2)}) copy-start(bf16[1,224,2048]{2,1,0:T(8,128)(2,1)} %param.14) | copy-start | bytes 2752516
  59.2 17.2 %collective-permute-start.5 = (bf16[896,256]{1,0:T(8,128)(2,1)S(1)}, bf16[896,256]{1,0:T(8,128)(2,1)S(1)}, u32[]{:S(2)}, u32[]{:S(2)}) collective-permute-start(bf16[896,256]{1,0:T(8,128)(2,1)S(1)} %shard_map.101.refs_2_), channel_id=1, source_target_pairs={{0,32},{32,64},{64,96},{96,0},{1,33},{33,65},{65,97},{97,1},{2,34}... | collective-permute-start | bytes 1376264 | tf_op jit(solution)/shard_map/ppermute | solution.py:152
  62.7 14.0 %collective-permute-start.7 = (bf16[896,256]{1,0:T(8,128)(2,1)S(1)}, bf16[896,256]{1,0:T(8,128)(2,1)S(1)}, u32[]{:S(2)}, u32[]{:S(2)}) collective-permute-start(bf16[896,256]{1,0:T(8,128)(2,1)S(1)} %shard_map.101.refs_2_), channel_id=1, source_target_pairs={{0,96},{32,0},{64,32},{96,64},{1,97},{33,1},{65,33},{97,65},{2,98}... | collective-permute-start | bytes 1376264 | tf_op jit(solution)/shard_map/ppermute | solution.py:153
  78.9 36.1 %all-to-all-start.2 = ((bf16[16,24,1024]{2,1,0:T(8,128)(2,1)}), bf16[16,24,1024]{2,1,0:T(8,128)(2,1)S(1)}, u32[]{:S(2)}, u32[]{:S(2)}) async-start(bf16[16,24,1024]{2,1,0:T(8,128)(2,1)} %bitcast.9.refs_7_), calls=%async_computation.2 | async-start | bytes 1572864 | tf_op jit(solution)/shard_map/all_to_all | solution.py:16
  85.1 14.1 %collective-permute-start.6 = (bf16[448,256]{1,0:T(8,128)(2,1)S(1)}, bf16[448,256]{1,0:T(8,128)(2,1)S(1)}, u32[]{:S(2)}, u32[]{:S(2)}) collective-permute-start(bf16[448,256]{1,0:T(8,128)(2,1)S(1)} %slice.56), channel_id=1, source_target_pairs={{0,32},{32,64},{64,96},{96,0},{1,33},{33,65},{65,97},{97,1},{2,34}... | collective-permute-start | bytes 688136 | tf_op jit(solution)/shard_map/ppermute | solution.py:155
  88.4 11.1 %collective-permute-start.8 = (bf16[448,256]{1,0:T(8,128)(2,1)S(1)}, bf16[448,256]{1,0:T(8,128)(2,1)S(1)}, u32[]{:S(2)}, u32[]{:S(2)}) collective-permute-start(bf16[448,256]{1,0:T(8,128)(2,1)S(1)} %slice.57), channel_id=1, source_target_pairs={{0,96},{32,0},{64,32},{96,64},{1,97},{33,1},{65,33},{97,65},{2,98}... | collective-permute-start | bytes 688136 | tf_op jit(solution)/shard_map/ppermute | solution.py:156
  99.5 1.6 copy-start
  101.1 10.5 %copy-start.7 = (bf16[1,2048,224]{1,2,0:T(8,128)(2,1)S(1)}, bf16[1,2048,224]{1,2,0:T(8,128)(2,1)}, u32[]{:S(2)}) copy-start(bf16[1,2048,224]{1,2,0:T(8,128)(2,1)} %param.16) | copy-start | bytes 2752516
  102.9 5.5 %collective-permute-start.11 = (bf16[256,512]{1,0:T(8,128)(2,1)S(1)}, bf16[256,512]{1,0:T(8,128)(2,1)S(1)}, u32[]{:S(2)}, u32[]{:S(2)}) collective-permute-start(bf16[256,512]{1,0:T(8,128)(2,1)S(1)} %get-tuple-element.8), channel_id=1, source_target_pairs={{0,16},{16,0},{1,17},{17,1},{2,18},{18,2},{3,19},{19,3},{4,20},{20... | collective-permute-start | bytes 786440 | tf_op jit(solution)/shard_map/ppermute | solution.py:24
  108.5 14.3 %collective-permute-start.12 = (bf16[256,512]{1,0:T(8,128)(2,1)S(1)}, bf16[256,512]{1,0:T(8,128)(2,1)}, u32[]{:S(2)}, u32[]{:S(2)}) collective-permute-start(bf16[256,512]{1,0:T(8,128)(2,1)S(1)} %fusion.3), channel_id=1, source_target_pairs={{0,1},{1,0},{2,3},{3,2},{4,5},{5,4},{6,7},{7,6},{8,9},{9,8},{10,11... | collective-permute-start | bytes 786440 | tf_op jit(solution)/shard_map/ppermute | solution.py:24
  112.5 12.1 %collective-permute-start.13 = (bf16[224,1024]{1,0:T(8,128)(2,1)}, bf16[224,1024]{1,0:T(8,128)(2,1)S(1)}, u32[]{:S(2)}, u32[]{:S(2)}) collective-permute-start(bf16[224,1024]{1,0:T(8,128)(2,1)} %broadcast_select_fusion.2), channel_id=1, source_target_pairs={{0,16},{16,0},{1,17},{17,1},{2,18},{18,2},{3,19},{19,3},{4,20},{20... | collective-permute-start | bytes 1376264 | tf_op jit(solution)/shard_map/ppermute | solution.py:24
  116.0 8.6 %copy-start.8 = (bf16[1,2048,224]{1,2,0:T(8,128)(2,1)S(1)}, bf16[1,2048,224]{1,2,0:T(8,128)(2,1)}, u32[]{:S(2)}) copy-start(bf16[1,2048,224]{1,2,0:T(8,128)(2,1)} %param.16) | copy-start | bytes 2752516
  116.0 22.6 %all-to-all-start.3 = ((bf16[16,12,1024]{2,1,0:T(8,128)(2,1)}), bf16[16,12,1024]{2,1,0:T(8,128)(2,1)S(1)}, u32[]{:S(2)}, u32[]{:S(2)}) async-start(bf16[16,12,1024]{2,1,0:T(8,128)(2,1)} %shard_map.106), calls=%async_computation.3 | async-start | bytes 1048576 | tf_op jit(solution)/shard_map/all_to_all | solution.py:16
  122.7 57.0 %all-gather.5.cloned.1.call-start = ((), (), s32[]{:S(2)}) async-start(), calls=%async_computation.7 | async-start | bytes 1179648 | tf_op jit(solution)/shard_map/all_gather | solution.py:168
  138.7 9.9 %copy-start.12 = (f32[1,16,6]{1,0,2:T(1,128)S(1)}, f32[1,16,6]{1,0,2:T(1,128)}, u32[]{:S(2)}) copy-start(f32[1,16,6]{1,0,2:T(1,128)} %param.19) | copy-start | bytes 1156
  138.7 9.9 %copy-start.13 = (s32[1,16]{1,0:T(1,128)S(1)}, s32[1,16]{1,0:T(1,128)}, u32[]{:S(2)}) copy-start(s32[1,16]{1,0:T(1,128)} %param.18) | copy-start | bytes 196
  139.2 40.5 %copy-start.1 = (bf16[2048,448]{0,1:T(8,128)(2,1)S(1)}, bf16[2048,448]{0,1:T(8,128)(2,1)}, u32[]{:S(2)}) copy-start(bf16[2048,448]{0,1:T(8,128)(2,1)} %param.13) | copy-start | bytes 5505028
  140.1 19.6 %all-to-all-start.4 = ((bf16[32,8,448]{2,1,0:T(8,128)(2,1)}), bf16[32,8,448]{2,1,0:T(8,128)(2,1)S(1)}, u32[]{:S(2)}, u32[]{:S(2)}) async-start(bf16[32,8,448]{2,1,0:T(8,128)(2,1)} %pad.22), calls=%async_computation.4 | async-start | bytes 524288 | tf_op jit(solution)/shard_map/all_to_all | solution.py:16
  179.7 1.2 copy-start.2
Sparse Core Ops, SparseCore 0:
  18.7 40.9 all-gather.2
  125.6 37.2 all-gather.4

commit v4 on v3

--- a/solution.py
+++ b/solution.py
@@ -55,6 +55,11 @@
 
 def pick_kernel(spread, tokens_t, out):
     out[...] = dot_t(spread[...], tokens_t[...]).astype(bf16)
+
+
+def halves_kernel(place, rows, own, send):
+    for core, out in ((place[0], own), (1 - place[0], send)):
+        out[...] = rows[:, pl.ds(pl.multiple_of(core * 1024, 1024), 1024)]
 
 
 def double_kernel(rows, out):
@@ -138,12 +143,17 @@
         return jnp.concatenate(
             [jnp.where(first, own, got), jnp.where(first, got, own)], axis=0)
 
-    g_w, u_w = chip_rows(expert_gate[0]), chip_rows(expert_up[0])
-    d_w = chip_rows(expert_down[0].T)
-
     ids = jnp.pad(hit_rows[0], ((0, 0), (0, 2)), constant_values=-1).reshape(128)
     spread = (ids[:, None] == jnp.arange(256, dtype=jnp.int32)[None, :]).astype(bf16)
     picked = call(pick_kernel, [((128, 448), bf16)], spread, tokens.T)[0].reshape(16, 8, 448)
+    g_own, g_send = call(halves_kernel, [((224, 1024), bf16)] * 2,
+                         core.reshape(1).astype(jnp.int32), expert_gate[0], scalars=1,
+                         after=[picked])
+    g_got = swap(g_send, "c")
+    g_w = jnp.concatenate(
+        [jnp.where(first, g_own, g_got), jnp.where(first, g_got, g_own)], axis=0)
+    u_w, d_w = chip_rows(expert_up[0]), chip_rows(expert_down[0].T)
+
     mine = exchange(picked, EXP)
     tok = call(stack_kernel, [((512, 256), bf16)], tok_own, tok_other)[0]
     tok = lax.all_gather(tok, "y", axis=0, tiled=True).reshape(8, 512, 256)

time: 190 us -> 190 us (level)
  waiting for transfers between devices: 46.4 us -> 44.2 us
    all_to_all x5, waiting for transfers between devices: 30.2 us -> 27.9 us  [exchange(): return lax.all_to_all(v, axes, 0, 0, tiled=True)]
    pallas_call x7 -> x8, Pallas kernels: 7.35 us -> 8.2 us  [call(): pl.pallas_call(run, out_shape=[jax.ShapeDtypeStruct(*v) for v in shapes],...]
where the time goes in v4:
time: 190 us; the launch traced here: 189 us
  starting transfers between devices  89.4 us (47%)
  waiting for transfers between devices  44.2 us (23%)
  blocking collectives  19.8 us (10%)
  between operations  14 us (7%)
  Pallas kernels  9.62 us (5%)
  other arithmetic  6.33 us (3%)
  local copies, waits for them, and re-layouts  5.52 us (3%)
    all_to_all x5, starting transfers between devices, exchange(): return lax.all_to_all(v, axes, 0, 0, tiled=True)  41.9 us
    all_to_all x5, waiting for transfers between devices, exchange(): return lax.all_to_all(v, axes, 0, 0, tiled=True)  27.9 us
    ppermute x6, starting transfers between devices, swap(): return lax.ppermute(v, axis, [(0, 1), (1, 0)])  23.5 us
    all_to_all x1, blocking collectives, exchange(): return lax.all_to_all(v, axes, 0, 0, tiled=True)  19.8 us
    ppermute x3, starting transfers between devices, body(): lax.ppermute(w, 'z', [(i, (i + s) % 4) for i in range(4)])  10.2 us
    pallas_call x8, Pallas kernels, call(): pl.pallas_call(run, out_shape=[jax.ShapeDtypeStruct(*v) for v in shapes],...  8.2 us
    ppermute x1, waiting for transfers between devices, body(): lax.ppermute(left[:448], 'x', [(i, (i + 1) % 4) for i in range(4)])  7.52 us
    ppermute x1, waiting for transfers between devices, body(): left = lax.ppermute(w, 'x', [(i, (i + 1) % 4) for i in range(4)])  5.92 us
  transfers between devices with their start and end apart: 21, of which 10 were waited for; matrix products, arithmetic and copies ran while one was open for 4% of the time, Pallas kernels for 4%

profile of v4, /device:TPU:1, one launch (start us, length us, event | category | flops | bytes accessed | tf_op | source)
XLA Modules:
  0.0 189.2 jit_solution(14500081159950788985)
XLA Ops:
  6.5 1.0 fusion.8
  7.9 8.9 %collective-permute-start = (bf16[256,256]{1,0:T(8,128)(2,1)S(1)}, bf16[256,256]{1,0:T(8,128)(2,1)S(1)}, u32[]{:S(2)}, u32[]{:S(2)}) collective-permute-start(bf16[256,256]{1,0:T(8,128)(2,1)S(1)} %pad.20), channel_id=1, source_target_pairs={{0,16},{16,0},{1,17},{17,1},{2,18},{18,2},{3,19},{19,3},{4,20},{20... | collective-permute-start | bytes 393224 | tf_op jit(solution)/shard_map/ppermute | solution.py:24
  16.9 0.9 collective-permute-done.refs_1_
  17.8 0.7 shard_map.100
  18.6 2.3 %collective-permute-start.10 = (bf16[224,1024]{1,0:T(8,128)(2,1)S(1)}, bf16[224,1024]{1,0:T(8,128)(2,1)S(1)}, u32[]{:S(2)}, u32[]{:S(2)}) collective-permute-start(bf16[224,1024]{1,0:T(8,128)(2,1)S(1)} %broadcast_select_fusion.6), channel_id=1, source_target_pairs={{0,16},{16,0},{1,17},{17,1},{2,18},{18,2},{3,19},{19,3},{4,20},{20... | collective-permute-start | bytes 1376264 | tf_op jit(solution)/shard_map/ppermute | solution.py:24
  21.0 0.7 collective-permute-start.1
  21.9 0.9 shard_map.102
  22.8 11.2 %all-to-all-start = ((bf16[16,8,448]{2,1,0:T(8,128)(2,1)}), bf16[16,8,448]{2,1,0:T(8,128)(2,1)S(1)}, u32[]{:S(2)}, u32[]{:S(2)}) async-start(bf16[16,8,448]{2,1,0:T(8,128)(2,1)} %bitcast.4.refs_2_), calls=%async_computation | async-start | bytes 262144 | tf_op jit(solution)/shard_map/all_to_all | solution.py:16
  34.1 0.8 shard_map.104
  34.9 2.3 %collective-permute-start.9 = (bf16[224,1024]{1,0:T(8,128)(2,1)}, bf16[224,1024]{1,0:T(8,128)(2,1)}, u32[]{:S(2)}, u32[]{:S(2)}) collective-permute-start(bf16[224,1024]{1,0:T(8,128)(2,1)} %get-tuple-element.10), channel_id=1, source_target_pairs={{0,16},{16,0},{1,17},{17,1},{2,18},{18,2},{3,19},{19,3},{4,20},{20... | collective-permute-start | bytes 1376264 | tf_op jit(solution)/shard_map/ppermute | solution.py:24
  37.3 3.1 %collective-permute-start.2 = (bf16[224,256]{1,0:T(8,128)(2,1)S(1)}, bf16[224,256]{1,0:T(8,128)(2,1)S(1)}, u32[]{:S(2)}, u32[]{:S(2)}) collective-permute-start(bf16[224,256]{1,0:T(8,128)(2,1)S(1)} %collective-permute-done.1.refs_0_), channel_id=1, source_target_pairs={{0,128},{128,256},{256,384},{384,0},{1,129},{129,257},{257,385},{3... | collective-permute-start | bytes 344072 | tf_op jit(solution)/shard_map/ppermute | solution.py:137
  40.4 4.6 %collective-permute-start.3 = (bf16[224,256]{1,0:T(8,128)(2,1)S(1)}, bf16[224,256]{1,0:T(8,128)(2,1)S(1)}, u32[]{:S(2)}, u32[]{:S(2)}) collective-permute-start(bf16[224,256]{1,0:T(8,128)(2,1)S(1)} %collective-permute-done.1.refs_0_), channel_id=1, source_target_pairs={{0,256},{128,384},{256,0},{384,128},{1,257},{129,385},{257,1},{385... | collective-permute-start | bytes 344072 | tf_op jit(solution)/shard_map/ppermute | solution.py:137
  45.0 2.5 %collective-permute-start.4 = (bf16[224,256]{1,0:T(8,128)(2,1)S(1)}, bf16[224,256]{1,0:T(8,128)(2,1)S(1)}, u32[]{:S(2)}, u32[]{:S(2)}) collective-permute-start(bf16[224,256]{1,0:T(8,128)(2,1)S(1)} %collective-permute-done.1.refs_0_), channel_id=1, source_target_pairs={{0,384},{128,0},{256,128},{384,256},{1,385},{129,1},{257,129},{385... | collective-permute-start | bytes 344072 | tf_op jit(solution)/shard_map/ppermute | solution.py:137
  47.5 1.1 all-to-all-done.refs_0_
  48.6 0.7 shard_map.103
  49.3 9.1 %all-to-all-start.1 = ((bf16[32,8,448]{2,1,0:T(8,128)(2,1)}), bf16[32,8,448]{2,1,0:T(8,128)(2,1)S(1)}, u32[]{:S(2)}, u32[]{:S(2)}) async-start(bf16[32,8,448]{2,1,0:T(8,128)(2,1)} %bitcast.5), calls=%async_computation.1 | async-start | bytes 524288 | tf_op jit(solution)/shard_map/all_to_all | solution.py:16
  58.5 3.3 %collective-permute-start.5 = (bf16[896,256]{1,0:T(8,128)(2,1)S(1)}, bf16[896,256]{1,0:T(8,128)(2,1)S(1)}, u32[]{:S(2)}, u32[]{:S(2)}) collective-permute-start(bf16[896,256]{1,0:T(8,128)(2,1)S(1)} %shard_map.101.refs_2_), channel_id=1, source_target_pairs={{0,32},{32,64},{64,96},{96,0},{1,33},{33,65},{65,97},{97,1},{2,34}... | collective-permute-start | bytes 1376264 | tf_op jit(solution)/shard_map/ppermute | solution.py:162
  61.8 3.2 %collective-permute-start.7 = (bf16[896,256]{1,0:T(8,128)(2,1)S(1)}, bf16[896,256]{1,0:T(8,128)(2,1)S(1)}, u32[]{:S(2)}, u32[]{:S(2)}) collective-permute-start(bf16[896,256]{1,0:T(8,128)(2,1)S(1)} %shard_map.101.refs_2_), channel_id=1, source_target_pairs={{0,96},{32,0},{64,32},{96,64},{1,97},{33,1},{65,33},{97,65},{2,98}... | collective-permute-start | bytes 1376264 | tf_op jit(solution)/shard_map/ppermute | solution.py:163
  65.0 1.2 broadcast_select_fusion.5
  66.3 1.1 broadcast_select_fusion.9
  67.5 2.1 %all-to-all-done.1 = bf16[32,8,448]{2,1,0:T(8,128)(2,1)S(1)} async-done(((bf16[32,8,448]{2,1,0:T(8,128)(2,1)}), bf16[32,8,448]{2,1,0:T(8,128)(2,1)S(1)}, u32[]{:S(2)}, u32[]{:S(2)}) %all-to-all-start.1) | async-done | bytes 229408 | tf_op jit(solution)/shard_map/all_to_all | solution.py:16
  69.7 5.9 %collective-permute-done.5.refs_3_ = bf16[896,256]{1,0:T(8,128)(2,1)S(1)} collective-permute-done((bf16[896,256]{1,0:T(8,128)(2,1)S(1)}, bf16[896,256]{1,0:T(8,128)(2,1)S(1)}, u32[]{:S(2)}, u32[]{:S(2)}) %collective-permute-start.5) | collective-permute-done | bytes 458784 | tf_op jit(solution)/shard_map/ppermute | solution.py:162
  75.6 0.4 collective-permute-done.7.refs_4_.refs_6_
  76.0 2.3 %shard_map.105 = bf16[384,1024]{1,0:T(8,128)(2,1)} custom-call(bf16[256,448]{1,0:T(8,128)(2,1)S(1)} %bitcast.30, bf16[448,1024]{1,0:T(8,128)(2,1)S(1)} %get-tuple-element.25.refs_1_, bf16[448,1024]{1,0:T(8,128)(2,1)S(1)} %get-tuple-element.26.refs_2_, bf16[896,256]{1,0:T(8,128)(2,1)S(1)} %collective-permute-done.5.refs_3_, ...), custom_call_target="tpu_custom_call" | custom-call | tf_op jit(solution)/shard_map/pallas_call | solution.py:44
  78.3 5.9 %all-to-all-start.2 = ((bf16[16,24,1024]{2,1,0:T(8,128)(2,1)}), bf16[16,24,1024]{2,1,0:T(8,128)(2,1)S(1)}, u32[]{:S(2)}, u32[]{:S(2)}) async-start(bf16[16,24,1024]{2,1,0:T(8,128)(2,1)} %bitcast.10.refs_7_), calls=%async_computation.2 | async-start | bytes 1572864 | tf_op jit(solution)/shard_map/all_to_all | solution.py:16
  84.3 3.3 %collective-permute-start.6 = (bf16[448,256]{1,0:T(8,128)(2,1)S(1)}, bf16[448,256]{1,0:T(8,128)(2,1)S(1)}, u32[]{:S(2)}, u32[]{:S(2)}) collective-permute-start(bf16[448,256]{1,0:T(8,128)(2,1)S(1)} %slice.48), channel_id=1, source_target_pairs={{0,32},{32,64},{64,96},{96,0},{1,33},{33,65},{65,97},{97,1},{2,34}... | collective-permute-start | bytes 688136 | tf_op jit(solution)/shard_map/ppermute | solution.py:165
  87.6 3.2 %collective-permute-start.8 = (bf16[448,256]{1,0:T(8,128)(2,1)S(1)}, bf16[448,256]{1,0:T(8,128)(2,1)S(1)}, u32[]{:S(2)}, u32[]{:S(2)}) collective-permute-start(bf16[448,256]{1,0:T(8,128)(2,1)S(1)} %slice.49), channel_id=1, source_target_pairs={{0,96},{32,0},{64,32},{96,64},{1,97},{33,1},{65,33},{97,65},{2,98}... | collective-permute-start | bytes 688136 | tf_op jit(solution)/shard_map/ppermute | solution.py:166
  90.9 7.5 %collective-permute-done.6.refs_4_ = bf16[448,256]{1,0:T(8,128)(2,1)S(1)} collective-permute-done((bf16[448,256]{1,0:T(8,128)(2,1)S(1)}, bf16[448,256]{1,0:T(8,128)(2,1)S(1)}, u32[]{:S(2)}, u32[]{:S(2)}) %collective-permute-start.6) | collective-permute-done | bytes 229408 | tf_op jit(solution)/shard_map/ppermute | solution.py:165
  98.7 1.6 copy-done
  100.3 1.8 shard_map.106
  102.1 4.4 %collective-permute-start.11 = (bf16[256,512]{1,0:T(8,128)(2,1)S(1)}, bf16[256,512]{1,0:T(8,128)(2,1)S(1)}, u32[]{:S(2)}, u32[]{:S(2)}) collective-permute-start(bf16[256,512]{1,0:T(8,128)(2,1)S(1)} %get-tuple-element.12), channel_id=1, source_target_pairs={{0,16},{16,0},{1,17},{17,1},{2,18},{18,2},{3,19},{19,3},{4,20},{20... | collective-permute-start | bytes 786440 | tf_op jit(solution)/shard_map/ppermute | solution.py:24
  106.4 1.1 collective-permute-done.11
  107.6 0.8 fusion.3
  108.4 3.1 %collective-permute-start.12 = (bf16[256,512]{1,0:T(8,128)(2,1)}, bf16[256,512]{1,0:T(8,128)(2,1)}, u32[]{:S(2)}, u32[]{:S(2)}) collective-permute-start(bf16[256,512]{1,0:T(8,128)(2,1)} %fusion.3), channel_id=1, source_target_pairs={{0,1},{1,0},{2,3},{3,2},{4,5},{5,4},{6,7},{7,6},{8,9},{9,8},{10,11... | collective-permute-start | bytes 786440 | tf_op jit(solution)/shard_map/ppermute | solution.py:24
  111.5 0.8 broadcast_select_fusion.2
  112.3 2.5 %collective-permute-start.13 = (bf16[224,1024]{1,0:T(8,128)(2,1)}, bf16[224,1024]{1,0:T(8,128)(2,1)S(1)}, u32[]{:S(2)}, u32[]{:S(2)}) collective-permute-start(bf16[224,1024]{1,0:T(8,128)(2,1)} %broadcast_select_fusion.2), channel_id=1, source_target_pairs={{0,16},{16,0},{1,17},{17,1},{2,18},{18,2},{3,19},{19,3},{4,20},{20... | collective-permute-start | bytes 1376264 | tf_op jit(solution)/shard_map/ppermute | solution.py:24
  114.9 1.0 shard_map.107
  115.8 6.7 %all-to-all-start.3 = ((bf16[16,12,1024]{2,1,0:T(8,128)(2,1)}), bf16[16,12,1024]{2,1,0:T(8,128)(2,1)S(1)}, u32[]{:S(2)}, u32[]{:S(2)}) async-start(bf16[16,12,1024]{2,1,0:T(8,128)(2,1)} %shard_map.107), calls=%async_computation.3 | async-start | bytes 1048576 | tf_op jit(solution)/shard_map/all_to_all | solution.py:16
  122.6 1.0 convert_add_fusion
  123.7 0.7 pad_maximum_fusion.2
  124.5 13.8 %all-to-all-done.3 = bf16[16,12,1024]{2,1,0:T(8,128)(2,1)S(1)} async-done(((bf16[16,12,1024]{2,1,0:T(8,128)(2,1)}), bf16[16,12,1024]{2,1,0:T(8,128)(2,1)S(1)}, u32[]{:S(2)}, u32[]{:S(2)}) %all-to-all-start.3) | async-done | bytes 393248 | tf_op jit(solution)/shard_map/all_to_all | solution.py:16
  138.4 0.5 convolution_convert_fusion
  139.0 0.8 pad.22
  139.7 8.9 %all-to-all-start.4 = ((bf16[32,8,448]{2,1,0:T(8,128)(2,1)}), bf16[32,8,448]{2,1,0:T(8,128)(2,1)S(1)}, u32[]{:S(2)}, u32[]{:S(2)}) async-start(bf16[32,8,448]{2,1,0:T(8,128)(2,1)} %pad.22), calls=%async_computation.4 | async-start | bytes 524288 | tf_op jit(solution)/shard_map/all_to_all | solution.py:16
  148.9 10.9 %all-to-all-done.4 = bf16[32,8,448]{2,1,0:T(8,128)(2,1)S(1)} async-done(((bf16[32,8,448]{2,1,0:T(8,128)(2,1)}), bf16[32,8,448]{2,1,0:T(8,128)(2,1)S(1)}, u32[]{:S(2)}, u32[]{:S(2)}) %all-to-all-start.4) | async-done | bytes 229408 | tf_op jit(solution)/shard_map/all_to_all | solution.py:16
  159.9 19.8 %all_to_all.30 = bf16[16,8,448]{2,1,0:T(8,128)(2,1)S(1)} all-to-all(bf16[16,8,448]{2,1,0:T(8,128)(2,1)S(1)} %multiply_convert_fusion), channel_id=1, replica_groups=mesh['z'=4,'x'=4,'c'=2,'y'=8,'h'=2] {'y','h'}, dimensions={0} | all-to-all | bytes 229376 | tf_op jit(solution)/shard_map/all_to_all | solution.py:16
  179.7 1.2 copy-done.2
  180.9 1.4 shard_map.108
  (64 shorter events, 2.0 us)
Async XLA Ops:
  6.5 12.0 %copy-start.5 = (bf16[1,224,2048]{2,1,0:T(8,128)(2,1)S(1)}, bf16[1,224,2048]{2,1,0:T(8,128)(2,1)}, u32[]{:S(2)}) copy-start(bf16[1,224,2048]{2,1,0:T(8,128)(2,1)} %param.15) | copy-start | bytes 2752516
  6.5 92.2 %all-gather.3.cloned.1.call-start = ((), (), s32[]{:S(2)}) async-start(), calls=%async_computation.6 | async-start | bytes 2359296 | tf_op jit(solution)/shard_map/all_gather | solution.py:159
  7.6 13.3 %copy-start.8 = (bf16[224,128]{1,0:T(8,128)(2,1)S(1)}, bf16[224,128]{1,0:T(8,128)(2,1)}, u32[]{:S(2)}) copy-start(bf16[224,128]{1,0:T(8,128)(2,1)} %param.12) | copy-start | bytes 172036
  7.6 13.3 %copy-start.9 = (bf16[224,128]{1,0:T(8,128)(2,1)S(1)}, bf16[224,128]{1,0:T(8,128)(2,1)}, u32[]{:S(2)}) copy-start(bf16[224,128]{1,0:T(8,128)(2,1)} %param.11) | copy-start | bytes 172036
  7.7 13.9 %copy-start.10 = (s32[1,16,6]{1,0,2:T(1,128)S(1)}, s32[1,16,6]{1,0,2:T(1,128)}, u32[]{:S(2)}) copy-start(s32[1,16,6]{1,0,2:T(1,128)} %param.17) | copy-start | bytes 1156
  7.8 14.1 %copy-start.3 = (bf16[256,448]{0,1:T(8,128)(2,1)S(1)}, bf16[256,448]{0,1:T(8,128)(2,1)}, u32[]{:S(2)}) copy-start(bf16[256,448]{0,1:T(8,128)(2,1)} %param.10) | copy-start | bytes 688132
  7.9 26.2 %copy-start.4 = (bf16[1,224,2048]{2,1,0:T(8,128)(2,1)S(1)}, bf16[1,224,2048]{2,1,0:T(8,128)(2,1)}, u32[]{:S(2)}) copy-start(bf16[1,224,2048]{2,1,0:T(8,128)(2,1)} %param.14) | copy-start | bytes 2752516
  7.9 9.9 %collective-permute-start = (bf16[256,256]{1,0:T(8,128)(2,1)S(1)}, bf16[256,256]{1,0:T(8,128)(2,1)S(1)}, u32[]{:S(2)}, u32[]{:S(2)}) collective-permute-start(bf16[256,256]{1,0:T(8,128)(2,1)S(1)} %pad.20), channel_id=1, source_target_pairs={{0,16},{16,0},{1,17},{17,1},{2,18},{18,2},{3,19},{19,3},{4,20},{20... | collective-permute-start | bytes 393224 | tf_op jit(solution)/shard_map/ppermute | solution.py:24
  18.6 46.4 %collective-permute-start.10 = (bf16[224,1024]{1,0:T(8,128)(2,1)S(1)}, bf16[224,1024]{1,0:T(8,128)(2,1)S(1)}, u32[]{:S(2)}, u32[]{:S(2)}) collective-permute-start(bf16[224,1024]{1,0:T(8,128)(2,1)S(1)} %broadcast_select_fusion.6), channel_id=1, source_target_pairs={{0,16},{16,0},{1,17},{17,1},{2,18},{18,2},{3,19},{19,3},{4,20},{20... | collective-permute-start | bytes 1376264 | tf_op jit(solution)/shard_map/ppermute | solution.py:24
  21.0 16.3 %collective-permute-start.1 = (bf16[224,256]{1,0:T(8,128)(2,1)S(1)}, bf16[224,256]{1,0:T(8,128)(2,1)S(1)}, u32[]{:S(2)}, u32[]{:S(2)}) collective-permute-start(bf16[224,256]{1,0:T(8,128)(2,1)S(1)} %pad_maximum_fusion.3), channel_id=1, source_target_pairs={{0,0},{1,32},{32,1},{33,33},{64,64},{65,96},{96,65},{97,97},{2,2},... | collective-permute-start | bytes 344072 | tf_op jit(solution)/shard_map/ppermute | solution.py:136
  22.8 25.8 %all-to-all-start = ((bf16[16,8,448]{2,1,0:T(8,128)(2,1)}), bf16[16,8,448]{2,1,0:T(8,128)(2,1)S(1)}, u32[]{:S(2)}, u32[]{:S(2)}) async-start(bf16[16,8,448]{2,1,0:T(8,128)(2,1)} %bitcast.4.refs_2_), calls=%async_computation | async-start | bytes 262144 | tf_op jit(solution)/shard_map/all_to_all | solution.py:16
  34.9 31.4 %collective-permute-start.9 = (bf16[224,1024]{1,0:T(8,128)(2,1)}, bf16[224,1024]{1,0:T(8,128)(2,1)}, u32[]{:S(2)}, u32[]{:S(2)}) collective-permute-start(bf16[224,1024]{1,0:T(8,128)(2,1)} %get-tuple-element.10), channel_id=1, source_target_pairs={{0,16},{16,0},{1,17},{17,1},{2,18},{18,2},{3,19},{19,3},{4,20},{20... | collective-permute-start | bytes 1376264 | tf_op jit(solution)/shard_map/ppermute | solution.py:24
  37.3 21.2 %collective-permute-start.2 = (bf16[224,256]{1,0:T(8,128)(2,1)S(1)}, bf16[224,256]{1,0:T(8,128)(2,1)S(1)}, u32[]{:S(2)}, u32[]{:S(2)}) collective-permute-start(bf16[224,256]{1,0:T(8,128)(2,1)S(1)} %collective-permute-done.1.refs_0_), channel_id=1, source_target_pairs={{0,128},{128,256},{256,384},{384,0},{1,129},{129,257},{257,385},{3... | collective-permute-start | bytes 344072 | tf_op jit(solution)/shard_map/ppermute | solution.py:137
  40.4 18.1 %collective-permute-start.3 = (bf16[224,256]{1,0:T(8,128)(2,1)S(1)}, bf16[224,256]{1,0:T(8,128)(2,1)S(1)}, u32[]{:S(2)}, u32[]{:S(2)}) collective-permute-start(bf16[224,256]{1,0:T(8,128)(2,1)S(1)} %collective-permute-done.1.refs_0_), channel_id=1, source_target_pairs={{0,256},{128,384},{256,0},{384,128},{1,257},{129,385},{257,1},{385... | collective-permute-start | bytes 344072 | tf_op jit(solution)/shard_map/ppermute | solution.py:137
  45.0 13.5 %collective-permute-start.4 = (bf16[224,256]{1,0:T(8,128)(2,1)S(1)}, bf16[224,256]{1,0:T(8,128)(2,1)S(1)}, u32[]{:S(2)}, u32[]{:S(2)}) collective-permute-start(bf16[224,256]{1,0:T(8,128)(2,1)S(1)} %collective-permute-done.1.refs_0_), channel_id=1, source_target_pairs={{0,384},{128,0},{256,128},{384,256},{1,385},{129,1},{257,129},{385... | collective-permute-start | bytes 344072 | tf_op jit(solution)/shard_map/ppermute | solution.py:137
  49.3 20.3 %all-to-all-start.1 = ((bf16[32,8,448]{2,1,0:T(8,128)(2,1)}), bf16[32,8,448]{2,1,0:T(8,128)(2,1)S(1)}, u32[]{:S(2)}, u32[]{:S(2)}) async-start(bf16[32,8,448]{2,1,0:T(8,128)(2,1)} %bitcast.5), calls=%async_computation.1 | async-start | bytes 524288 | tf_op jit(solution)/shard_map/all_to_all | solution.py:16
  58.5 17.1 %collective-permute-start.5 = (bf16[896,256]{1,0:T(8,128)(2,1)S(1)}, bf16[896,256]{1,0:T(8,128)(2,1)S(1)}, u32[]{:S(2)}, u32[]{:S(2)}) collective-permute-start(bf16[896,256]{1,0:T(8,128)(2,1)S(1)} %shard_map.101.refs_2_), channel_id=1, source_target_pairs={{0,32},{32,64},{64,96},{96,0},{1,33},{33,65},{65,97},{97,1},{2,34}... | collective-permute-start | bytes 1376264 | tf_op jit(solution)/shard_map/ppermute | solution.py:162
  61.8 14.2 %collective-permute-start.7 = (bf16[896,256]{1,0:T(8,128)(2,1)S(1)}, bf16[896,256]{1,0:T(8,128)(2,1)S(1)}, u32[]{:S(2)}, u32[]{:S(2)}) collective-permute-start(bf16[896,256]{1,0:T(8,128)(2,1)S(1)} %shard_map.101.refs_2_), channel_id=1, source_target_pairs={{0,96},{32,0},{64,32},{96,64},{1,97},{33,1},{65,33},{97,65},{2,98}... | collective-permute-start | bytes 1376264 | tf_op jit(solution)/shard_map/ppermute | solution.py:163
  78.3 36.6 %all-to-all-start.2 = ((bf16[16,24,1024]{2,1,0:T(8,128)(2,1)}), bf16[16,24,1024]{2,1,0:T(8,128)(2,1)S(1)}, u32[]{:S(2)}, u32[]{:S(2)}) async-start(bf16[16,24,1024]{2,1,0:T(8,128)(2,1)} %bitcast.10.refs_7_), calls=%async_computation.2 | async-start | bytes 1572864 | tf_op jit(solution)/shard_map/all_to_all | solution.py:16
  84.3 14.1 %collective-permute-start.6 = (bf16[448,256]{1,0:T(8,128)(2,1)S(1)}, bf16[448,256]{1,0:T(8,128)(2,1)S(1)}, u32[]{:S(2)}, u32[]{:S(2)}) collective-permute-start(bf16[448,256]{1,0:T(8,128)(2,1)S(1)} %slice.48), channel_id=1, source_target_pairs={{0,32},{32,64},{64,96},{96,0},{1,33},{33,65},{65,97},{97,1},{2,34}... | collective-permute-start | bytes 688136 | tf_op jit(solution)/shard_map/ppermute | solution.py:165
  87.6 11.1 %collective-permute-start.8 = (bf16[448,256]{1,0:T(8,128)(2,1)S(1)}, bf16[448,256]{1,0:T(8,128)(2,1)S(1)}, u32[]{:S(2)}, u32[]{:S(2)}) collective-permute-start(bf16[448,256]{1,0:T(8,128)(2,1)S(1)} %slice.49), channel_id=1, source_target_pairs={{0,96},{32,0},{64,32},{96,64},{1,97},{33,1},{65,33},{97,65},{2,98}... | collective-permute-start | bytes 688136 | tf_op jit(solution)/shard_map/ppermute | solution.py:166
  98.7 1.6 copy-start
  100.3 11.2 %copy-start.6 = (bf16[1,2048,224]{1,2,0:T(8,128)(2,1)S(1)}, bf16[1,2048,224]{1,2,0:T(8,128)(2,1)}, u32[]{:S(2)}) copy-start(bf16[1,2048,224]{1,2,0:T(8,128)(2,1)} %param.16) | copy-start | bytes 2752516
  102.1 5.5 %collective-permute-start.11 = (bf16[256,512]{1,0:T(8,128)(2,1)S(1)}, bf16[256,512]{1,0:T(8,128)(2,1)S(1)}, u32[]{:S(2)}, u32[]{:S(2)}) collective-permute-start(bf16[256,512]{1,0:T(8,128)(2,1)S(1)} %get-tuple-element.12), channel_id=1, source_target_pairs={{0,16},{16,0},{1,17},{17,1},{2,18},{18,2},{3,19},{19,3},{4,20},{20... | collective-permute-start | bytes 786440 | tf_op jit(solution)/shard_map/ppermute | solution.py:24
  108.4 14.2 %collective-permute-start.12 = (bf16[256,512]{1,0:T(8,128)(2,1)}, bf16[256,512]{1,0:T(8,128)(2,1)}, u32[]{:S(2)}, u32[]{:S(2)}) collective-permute-start(bf16[256,512]{1,0:T(8,128)(2,1)} %fusion.3), channel_id=1, source_target_pairs={{0,1},{1,0},{2,3},{3,2},{4,5},{5,4},{6,7},{7,6},{8,9},{9,8},{10,11... | collective-permute-start | bytes 786440 | tf_op jit(solution)/shard_map/ppermute | solution.py:24
  112.3 12.1 %collective-permute-start.13 = (bf16[224,1024]{1,0:T(8,128)(2,1)}, bf16[224,1024]{1,0:T(8,128)(2,1)S(1)}, u32[]{:S(2)}, u32[]{:S(2)}) collective-permute-start(bf16[224,1024]{1,0:T(8,128)(2,1)} %broadcast_select_fusion.2), channel_id=1, source_target_pairs={{0,16},{16,0},{1,17},{17,1},{2,18},{18,2},{3,19},{19,3},{4,20},{20... | collective-permute-start | bytes 1376264 | tf_op jit(solution)/shard_map/ppermute | solution.py:24
  115.8 8.6 %copy-start.7 = (bf16[1,2048,224]{1,2,0:T(8,128)(2,1)S(1)}, bf16[1,2048,224]{1,2,0:T(8,128)(2,1)}, u32[]{:S(2)}) copy-start(bf16[1,2048,224]{1,2,0:T(8,128)(2,1)} %param.16) | copy-start | bytes 2752516
  115.8 22.5 %all-to-all-start.3 = ((bf16[16,12,1024]{2,1,0:T(8,128)(2,1)}), bf16[16,12,1024]{2,1,0:T(8,128)(2,1)S(1)}, u32[]{:S(2)}, u32[]{:S(2)}) async-start(bf16[16,12,1024]{2,1,0:T(8,128)(2,1)} %shard_map.107), calls=%async_computation.3 | async-start | bytes 1048576 | tf_op jit(solution)/shard_map/all_to_all | solution.py:16
  122.5 57.2 %all-gather.5.cloned.1.call-start = ((), (), s32[]{:S(2)}) async-start(), calls=%async_computation.7 | async-start | bytes 1179648 | tf_op jit(solution)/shard_map/all_gather | solution.py:178
  138.4 10.3 %copy-start.11 = (f32[1,16,6]{1,0,2:T(1,128)S(1)}, f32[1,16,6]{1,0,2:T(1,128)}, u32[]{:S(2)}) copy-start(f32[1,16,6]{1,0,2:T(1,128)} %param.19) | copy-start | bytes 1156
  138.4 10.3 %copy-start.12 = (s32[1,16]{1,0:T(1,128)S(1)}, s32[1,16]{1,0:T(1,128)}, u32[]{:S(2)}) copy-start(s32[1,16]{1,0:T(1,128)} %param.18) | copy-start | bytes 196
  138.9 40.8 %copy-start.1 = (bf16[2048,448]{0,1:T(8,128)(2,1)S(1)}, bf16[2048,448]{0,1:T(8,128)(2,1)}, u32[]{:S(2)}) copy-start(bf16[2048,448]{0,1:T(8,128)(2,1)} %param.13) | copy-start | bytes 5505028
  139.7 20.1 %all-to-all-start.4 = ((bf16[32,8,448]{2,1,0:T(8,128)(2,1)}), bf16[32,8,448]{2,1,0:T(8,128)(2,1)S(1)}, u32[]{:S(2)}, u32[]{:S(2)}) async-start(bf16[32,8,448]{2,1,0:T(8,128)(2,1)} %pad.22), calls=%async_computation.4 | async-start | bytes 524288 | tf_op jit(solution)/shard_map/all_to_all | solution.py:16
  179.7 1.2 copy-start.2
Sparse Core Ops, SparseCore 0:
  18.7 41.4 all-gather.2
  125.4 38.4 all-gather.4
